TPU v7x, 128 devices: a whole 4x4x4 slice. The times are simulated.
128 devices in a mesh: section: 4 (over y), expert: 32 (over x, z, core).
Axes of the slice: x: 4, y: 4, z: 4, core: 2. Of those that a mesh axis runs over, the one named last changes fastest.
Arguments:
- saved_inputs: bfloat16 [4, 2, 2048, 4096], P('section', None, 'expert'), may hold values from -6 to 6
- arriving: bfloat16 [4, 2048, 4096], P('section', 'expert'), may hold values from -1.5 to 1.5
- last_grad: bfloat16 [2048, 4096], P('expert'), may hold values from -1.5 to 1.5
- expert_ids: int32 [4, 2, 2048, 3], P('section', None, 'expert'), may hold values from 0 to 15, all different within a row; in each aligned block of 64 rows (0 to 63, 64 to 127, ..., all dimensions but the last counted through in order) at most 14 rows name the same one
- combine: bfloat16 [4, 2, 2048, 3], P('section', None, 'expert'), may hold values from 0.099609375 to 1
- w_gate: bfloat16 [4, 32, 4096, 384], P('section', 'expert'), may hold values from -0.09375 to 0.09375
- w_up: bfloat16 [4, 32, 4096, 384], P('section', 'expert'), may hold values from -0.09375 to 0.09375
- w_down: bfloat16 [4, 32, 384, 4096], P('section', 'expert'), may hold values from -0.21875 to 0.21875
Outputs:
- first_grads: bfloat16 [4, 2048, 4096], P('section', 'expert')
- second_grads: bfloat16 [4, 2048, 4096], P('section', 'expert')
- grad_gate: bfloat16 [4, 32, 4096, 384], P('section', 'expert')
- grad_up: bfloat16 [4, 32, 4096, 384], P('section', 'expert')
- grad_down: bfloat16 [4, 32, 384, 4096], P('section', 'expert')
Inputs may be any that keep to these rules, and one draw needn't show every extreme that they name: `expert_ids`: each token names 3 different experts. In every aligned block of 64 tokens (the tokens of one device in one section and micro-batch) no expert is named by more than 14 tokens, and in some blocks one expert is named by exactly 14.
All inputs are finite; a program needn't handle non-finite values.
Results may differ from a plain program's by a relative error of at most 0.0085.
Values may be sent and summed in bfloat16 or wider, within the bound.
A program may use at most 192 MiB of HBM per device.

v0:
```python
import jax
import jax.numpy as jnp
from jax import lax
from jax.sharding import PartitionSpec as P

HALVES = 2


def shifted(value, axis, by):
    count = lax.axis_size(axis)
    pairs = [(i, i + by) for i in range(count) if 0 <= i + by < count]
    return lax.ppermute(value, axis, pairs)


def rows_backward(x_rows, weighted, gate_w, up_w, down_w):
    gate_pre = jnp.dot(x_rows, gate_w, preferred_element_type=jnp.float32)
    up_pre = jnp.dot(x_rows, up_w, preferred_element_type=jnp.float32)
    gate_sigmoid = jax.nn.sigmoid(gate_pre)
    active = gate_pre * gate_sigmoid
    hidden = (active * up_pre).astype(jnp.bfloat16)
    contract = (((1,), (1,)), ((), ()))
    hidden_grad = lax.dot_general(weighted, down_w, contract, preferred_element_type=jnp.float32)
    gate_rows = (
        hidden_grad * up_pre * gate_sigmoid * (1.0 + gate_pre * (1.0 - gate_sigmoid))
    ).astype(jnp.bfloat16)
    up_rows = (hidden_grad * active).astype(jnp.bfloat16)
    partial_value = lax.dot_general(gate_rows, gate_w, contract, preferred_element_type=jnp.float32)
    partial_value = partial_value + lax.dot_general(
        up_rows, up_w, contract, preferred_element_type=jnp.float32
    )
    return (partial_value, hidden, gate_rows, up_rows)


def weight_terms(pieces):
    x_rows, weighted, hidden, gate_rows, up_rows = pieces
    across = (((0,), (0,)), ((), ()))
    return (
        lax.dot_general(x_rows, gate_rows, across, preferred_element_type=jnp.float32),
        lax.dot_general(x_rows, up_rows, across, preferred_element_type=jnp.float32),
        lax.dot_general(hidden, weighted, across, preferred_element_type=jnp.float32),
    )


def route_targets(route_ids, experts, capacity):
    tokens, top_count = route_ids.shape
    flat_ids = route_ids.reshape(tokens * top_count)
    onehot = (flat_ids[:, None] == jnp.arange(experts, dtype=jnp.int32)[None, :]).astype(jnp.int32)
    before = jnp.cumsum(onehot, axis=0) - onehot
    slot_index = jnp.sum(before * onehot, axis=1)
    return (flat_ids * capacity + slot_index).reshape(tokens, top_count)


def local(saved_inputs, arriving, last_grad, expert_ids, combine, w_gate, w_up, w_down):
    gate_w = w_gate[0, 0]
    up_w = w_up[0, 0]
    down_w = w_down[0, 0]
    tok_dev = arriving.shape[1]
    model_width = arriving.shape[2]
    top_count = expert_ids.shape[3]
    shards = lax.axis_size("expert")
    experts = shards // HALVES
    capacity = 5 * tok_dev * top_count // (4 * experts) // 2 * 2

    def section_pass(inputs, grads_in, route_ids, weights):
        target = route_targets(route_ids, experts, capacity)
        positions = jnp.arange(experts * capacity, dtype=jnp.int32)
        placed = target[None, :, :] == positions[:, None, None]
        picked = jnp.any(placed, axis=2).astype(jnp.bfloat16)
        scaled = jnp.sum(
            jnp.where(placed, weights[None, :, :].astype(jnp.float32), 0.0), axis=2
        ).astype(jnp.bfloat16)
        tables = jnp.stack([picked, scaled])
        sources = jnp.stack([inputs, grads_in])
        payload = jnp.einsum(
            "pqt,ptd->pqd", tables, sources, preferred_element_type=jnp.float32
        ).astype(jnp.bfloat16)
        spread = jnp.broadcast_to(
            payload.reshape(2, experts, 1, capacity, model_width),
            (2, experts, HALVES, capacity, model_width),
        )
        arrived = lax.all_to_all(
            spread.reshape(2, shards, capacity, model_width),
            "expert",
            split_axis=1,
            concat_axis=1,
            tiled=True,
        )
        x_rows = arrived[0].reshape(shards * capacity, model_width)
        weighted = arrived[1].reshape(shards * capacity, model_width)
        partial_value, hidden, gate_rows, up_rows = rows_backward(
            x_rows, weighted, gate_w, up_w, down_w
        )
        partial_value = partial_value.reshape(shards, capacity, model_width)
        returned_rows = lax.all_to_all(
            partial_value, "expert", split_axis=0, concat_axis=0, tiled=True
        )
        expert_rows = jnp.sum(
            returned_rows.reshape(experts, HALVES, capacity, model_width), axis=1
        ).astype(jnp.bfloat16)
        collect = jnp.any(target[:, :, None] == positions[None, None, :], axis=1).astype(
            jnp.bfloat16
        )
        expert_sum = jnp.dot(
            collect,
            expert_rows.reshape(experts * capacity, model_width),
            preferred_element_type=jnp.float32,
        )
        result = (grads_in.astype(jnp.float32) + expert_sum).astype(jnp.bfloat16)
        return (result, (x_rows, weighted, hidden, gate_rows, up_rows))

    section_last = lax.axis_index("section") == lax.axis_size("section") - 1
    first_grad, kept_first = section_pass(
        saved_inputs[0, 0], arriving[0], expert_ids[0, 0], combine[0, 0]
    )
    totals = weight_terms(kept_first)
    passed = shifted(first_grad, "section", -1)
    incoming = jnp.where(section_last, last_grad, passed)
    second_grad, kept_second = section_pass(
        saved_inputs[0, 1], incoming, expert_ids[0, 1], combine[0, 1]
    )
    second_terms = weight_terms(kept_second)
    totals = tuple((pair[0] + pair[1] for pair in zip(totals, second_terms)))
    return (
        first_grad[None],
        second_grad[None],
        totals[0].astype(jnp.bfloat16)[None, None],
        totals[1].astype(jnp.bfloat16)[None, None],
        totals[2].astype(jnp.bfloat16)[None, None],
    )


def solution(mesh):
    return jax.shard_map(
        local,
        mesh=mesh,
        in_specs=(
            P("section", None, "expert", None),
            P("section", "expert", None),
            P("expert", None),
            P("section", None, "expert", None),
            P("section", None, "expert", None),
            P("section", "expert", None, None),
            P("section", "expert", None, None),
            P("section", "expert", None, None),
        ),
        out_specs=(
            P("section", "expert", None),
            P("section", "expert", None),
            P("section", "expert", None, None),
            P("section", "expert", None, None),
            P("section", "expert", None, None),
        ),
        check_vma=False,
    )
```

profile of v0, /device:TPU:52, one launch (start us, length us, event | category | flops | bytes accessed | tf_op | source)
XLA Modules:
  0.0 666.0 jit_solution(7968685927313758433)
XLA Ops:
  0.6 0.9 broadcast_multiply_fusion
  1.5 0.1 copy.53
  1.6 0.1 eq.99
  1.8 0.6 reduce-window.14
  2.4 0.2 slice_reduce_fusion.5
  2.7 0.1 reduce_sum.59
  3.0 0.2 eq.113
  3.2 0.6 reduce-window.16
  3.8 0.2 slice_reduce_fusion.4
  4.1 0.1 reduce_sum.63
  4.3 0.8 slice_convert_fusion
  5.1 0.1 fusion.34
  5.2 0.1 select_reduce_fusion.1
  5.4 2.1 slice_bitcast_fusion
  7.4 2.2 convolution_convert_fusion.1
  9.6 3.8 copy.57
  13.5 7.1 %broadcast_in_dim.56 = bf16[2,16,2,14,4096]{4,0,3,2,1:T(2,128)(2,1)S(1)} broadcast(bf16[2,16,14,4096]{3,0,2,1:T(2,128)(2,1)S(1)} %bitcast.125), dimensions={0,1,3,4} | broadcast | bytes 11010048 | tf_op jit(solution)/shard_map/broadcast_in_dim | solution.py:77
  20.6 89.6 %all_to_all.20 = bf16[2,32,14,4096]{3,0,2,1:T(2,128)(2,1)S(1)} all-to-all(bf16[2,32,14,4096]{3,0,2,1:T(2,128)(2,1)S(1)} %bitcast.123), channel_id=1, replica_groups=mesh['section'=4,'expert'=32] {'expert'}, dimensions={1} | all-to-all | bytes 14680064 | tf_op jit(solution)/shard_map/all_to_all | solution.py:81
  110.2 36.9 %slice_reduce_fusion.3 = (bf16[32,14,4096]{2,1,0:T(8,128)(2,1)}, bf16[32,14,4096]{2,1,0:T(8,128)(2,1)}) fusion(bf16[2,32,14,4096]{3,0,2,1:T(2,128)(2,1)S(1)} %all_to_all.20), kind=kLoop, calls=%fused_computation.5 | loop fusion | bytes 14680064 | tf_op jit(solution)/shard_map/slice | solution.py:89
  147.1 5.0 reshape_squeeze.15
  152.1 5.1 fusion.10
  157.2 2.9 fusion.16
  160.1 5.1 reshape_squeeze.14
  165.2 5.5 multiply_convert_fusion.4
  170.8 2.1 fusion.8
  172.9 5.2 convolution_add_fusion.1
  178.1 6.9 %reshape.163 = f32[32,14,4096]{2,1,0:T(8,128)} reshape(f32[448,4096]{1,0:T(8,128)} %convolution_add_fusion.1) | data formatting | bytes 14680064 | tf_op jit(solution)/shard_map/reshape | solution.py:93
  184.9 8.0 %all-to-all-start.1 = ((f32[32,14,4096]{2,1,0:T(8,128)}), f32[32,14,4096]{2,1,0:T(8,128)}, u32[]{:S(2)}, u32[]{:S(2)}) async-start(f32[32,14,4096]{2,1,0:T(8,128)} %reshape.163), calls=%async_computation.1 | async-start | bytes 16777216 | tf_op jit(solution)/shard_map/all_to_all | solution.py:94
  193.0 0.1 fusion.35
  193.1 124.2 %all-to-all-done.1 = f32[32,14,4096]{2,1,0:T(8,128)} async-done(((f32[32,14,4096]{2,1,0:T(8,128)}), f32[32,14,4096]{2,1,0:T(8,128)}, u32[]{:S(2)}, u32[]{:S(2)}) %all-to-all-start.1) | async-done | bytes 7340064 | tf_op jit(solution)/shard_map/all_to_all | solution.py:94
  317.3 6.0 bitcast_reduce_fusion.1
  323.2 2.7 convert_element_type.159
  326.0 2.8 fusion.3
  328.8 2.6 collective-permute-start
  331.4 0.1 fusion.33
  331.5 0.1 select_reduce_fusion
  331.6 12.8 %collective-permute-done = bf16[64,4096]{1,0:T(8,128)(2,1)} collective-permute-done((bf16[64,4096]{1,0:T(8,128)(2,1)}, bf16[64,4096]{1,0:T(8,128)(2,1)}, u32[]{:S(2)}, u32[]{:S(2)}) %collective-permute-start) | collective-permute-done | bytes 524320 | tf_op jit(solution)/shard_map/ppermute | solution.py:12
  344.5 1.1 fusion.32
  345.6 2.2 convolution_convert_fusion
  347.8 3.8 copy.62
  351.6 7.1 %broadcast_in_dim.60 = bf16[2,16,2,14,4096]{4,0,3,2,1:T(2,128)(2,1)S(1)} broadcast(bf16[2,16,14,4096]{3,0,2,1:T(2,128)(2,1)S(1)} %bitcast.126), dimensions={0,1,3,4} | broadcast | bytes 11010048 | tf_op jit(solution)/shard_map/broadcast_in_dim | solution.py:77
  358.8 87.1 %all_to_all.21 = bf16[2,32,14,4096]{3,0,2,1:T(2,128)(2,1)S(1)} all-to-all(bf16[2,32,14,4096]{3,0,2,1:T(2,128)(2,1)S(1)} %bitcast.124), channel_id=1, replica_groups=mesh['section'=4,'expert'=32] {'expert'}, dimensions={1} | all-to-all | bytes 14680064 | tf_op jit(solution)/shard_map/all_to_all | solution.py:81
  445.9 36.9 %slice_reduce_fusion.1 = (bf16[32,14,4096]{2,1,0:T(8,128)(2,1)}, bf16[32,14,4096]{2,1,0:T(8,128)(2,1)}) fusion(bf16[2,32,14,4096]{3,0,2,1:T(2,128)(2,1)S(1)} %all_to_all.21), kind=kLoop, calls=%fused_computation.3 | loop fusion | bytes 14680064 | tf_op jit(solution)/shard_map/slice | solution.py:89
  482.8 5.0 reshape_squeeze.17
  487.8 6.1 fusion.13
  493.9 2.9 fusion.6
  496.8 5.4 reshape_squeeze.16
  502.2 5.5 multiply_convert_fusion.2
  507.7 2.1 fusion.4
  509.9 5.1 convolution_add_fusion
  515.0 6.8 %reshape.168 = f32[32,14,4096]{2,1,0:T(8,128)} reshape(f32[448,4096]{1,0:T(8,128)} %convolution_add_fusion) | data formatting | bytes 14680064 | tf_op jit(solution)/shard_map/reshape | solution.py:93
  521.8 8.2 %all-to-all-start.3 = ((f32[32,14,4096]{2,1,0:T(8,128)}), f32[32,14,4096]{2,1,0:T(8,128)}, u32[]{:S(2)}, u32[]{:S(2)}) async-start(f32[32,14,4096]{2,1,0:T(8,128)} %reshape.168), calls=%async_computation.3 | async-start | bytes 16777216 | tf_op jit(solution)/shard_map/all_to_all | solution.py:94
  530.0 0.1 fusion.36
  530.1 4.6 fusion.54
  534.8 2.5 fusion.53
  537.3 1.9 fusion.31
  539.2 0.1 copy-done.2
  539.4 4.2 fusion.1
  543.6 4.2 fusion
  547.9 3.9 fusion.2
  551.8 102.3 %all-to-all-done.3 = f32[32,14,4096]{2,1,0:T(8,128)} async-done(((f32[32,14,4096]{2,1,0:T(8,128)}), f32[32,14,4096]{2,1,0:T(8,128)}, u32[]{:S(2)}, u32[]{:S(2)}) %all-to-all-start.3) | async-done | bytes 7340064 | tf_op jit(solution)/shard_map/all_to_all | solution.py:94
  654.1 6.1 bitcast_reduce_fusion
  660.2 2.8 convert_element_type.173
  662.9 2.9 fusion.30
  (58 shorter events, 0.7 us)
Async XLA Ops:
  0.6 151.4 %copy-start = (bf16[1,1,4096,384]{3,2,1,0:T(8,128)(2,1)S(1)}, bf16[1,1,4096,384]{3,2,1,0:T(8,128)(2,1)}, u32[]{:S(2)}) copy-start(bf16[1,1,4096,384]{3,2,1,0:T(8,128)(2,1)} %param.13) | copy-start | bytes 9437188
  152.1 5.1 copy-start.3
  152.1 5.1 copy-start.7
  170.7 2.1 copy-start.12
  170.8 2.1 copy-start.8
  184.9 132.3 %all-to-all-start.1 = ((f32[32,14,4096]{2,1,0:T(8,128)}), f32[32,14,4096]{2,1,0:T(8,128)}, u32[]{:S(2)}, u32[]{:S(2)}) async-start(f32[32,14,4096]{2,1,0:T(8,128)} %reshape.163), calls=%async_computation.1 | async-start | bytes 16777216 | tf_op jit(solution)/shard_map/all_to_all | solution.py:94
  328.8 15.7 %collective-permute-start = (bf16[64,4096]{1,0:T(8,128)(2,1)}, bf16[64,4096]{1,0:T(8,128)(2,1)}, u32[]{:S(2)}, u32[]{:S(2)}) collective-permute-start(bf16[64,4096]{1,0:T(8,128)(2,1)} %fusion.3), channel_id=1, source_target_pairs={{32,0},{64,32},{96,64},{33,1},{65,33},{97,65},{34,2},{66,34},{98,6... | collective-permute-start | bytes 1572872 | tf_op jit(solution)/shard_map/ppermute | solution.py:12
  487.8 6.1 copy-start.1
  507.7 2.1 copy-start.14
  507.7 2.1 copy-start.10
  507.7 2.1 copy-start.9
  521.8 132.3 %all-to-all-start.3 = ((f32[32,14,4096]{2,1,0:T(8,128)}), f32[32,14,4096]{2,1,0:T(8,128)}, u32[]{:S(2)}, u32[]{:S(2)}) async-start(f32[32,14,4096]{2,1,0:T(8,128)} %reshape.168), calls=%async_computation.3 | async-start | bytes 16777216 | tf_op jit(solution)/shard_map/all_to_all | solution.py:94
  530.1 4.7 copy-start.4
  530.1 4.7 copy-start.13
  534.8 2.5 copy-start.5
  534.8 2.5 copy-start.16
  534.8 2.5 copy-start.17
  537.3 2.0 copy-start.2
  537.3 2.1 copy-start.11
  539.4 4.2 copy-start.15
  543.6 4.2 copy-start.6
  543.6 4.2 copy-start.18
  543.6 4.2 copy-start.19
where the time goes:
time: 672 us; the launch traced here: 666 us
  waiting for transfers between devices  239 us (36%)
  blocking collectives  177 us (26%)
  local copies, waits for them, and re-layouts  139 us (21%)
  matrix products  74 us (11%)
  starting transfers between devices  18.7 us (3%)
  other arithmetic  16.9 us (3%)
    all_to_all x2, waiting for transfers between devices, section_pass(): lax.all_to_all(partial_value, 'expert', split_axis=0, concat_axis=0, tile...  227 us
    all_to_all x2, blocking collectives, section_pass(): lax.all_to_all(spread.reshape(2, shards, capacity, model_width), 'expert'...  177 us
    slice x2, local copies, waits for them, and re-layouts, section_pass(): weighted = arrived[1].reshape(shards * capacity, model_width)  73.9 us
    all_to_all x2, starting transfers between devices, section_pass(): lax.all_to_all(partial_value, 'expert', split_axis=0, concat_axis=0, tile...  16.2 us
    broadcast_in_dim x2, local copies, waits for them, and re-layouts, section_pass(): jnp.broadcast_to(payload.reshape(2, experts, 1, capacity, model_width), (...  14.2 us
    reshape x2, local copies, waits for them, and re-layouts, section_pass(): partial_value = partial_value.reshape(shards, capacity, model_width)  13.7 us
  transfers between devices with their start and end apart: 3, of which 3 were waited for; matrix products, arithmetic and copies ran while one was open for 3% of the time, Pallas kernels for 0%

commit v1 on v0

v1 whole, which is shorter than its diff:
```python
import jax
import jax.numpy as jnp
from jax import lax
from jax.experimental import pallas as pl
from jax.experimental.pallas import tpu as pltpu
from jax.sharding import PartitionSpec as P

MESH = pl.DeviceIdType.MESH
F32 = jnp.float32
BF16 = jnp.bfloat16

RING = 4
PEERS = RING * RING
ROWS = 16
CAP = 14
GROUP = 512
FULL = 7
WIDE = FULL * GROUP
D = 4096
TOK = 64
FF = 384
ALL = PEERS * ROWS

ORDER = tuple(
    (dx % RING) * RING + dz % RING
    for dx, dz in (
        (2, 2), (1, 0), (-1, 0), (2, 1), (0, -1), (1, 2), (0, 1), (2, -1),
        (1, 1), (-1, 2), (-1, -1), (2, 0), (1, -1), (0, 2), (-1, 1),
    )
)

ACROSS = (((1,), (1,)), ((), ()))
DOWN = (((0,), (0,)), ((), ()))


def mm(a, b):
    return jnp.dot(a, b, preferred_element_type=F32)


def mm_t(a, b):
    return lax.dot_general(a, b, ACROSS, preferred_element_type=F32)


def iota(shape, axis):
    return lax.broadcasted_iota(jnp.int32, shape, axis)


def spread(group, transposed):
    to, come = iota((ALL, ALL), int(transposed)), iota((ALL, ALL), int(not transposed))
    slot = to % ROWS
    late = (slot >= 7).astype(jnp.int32)
    hit = jnp.logical_and(come == to - slot + CAP + late, slot - 7 * late == group)
    return hit.astype(F32).astype(BF16)


def cols(group):
    return pl.ds(pl.multiple_of(group * GROUP, GROUP), GROUP)


def kernel(
    x_ref, dy_ref, last_ref, ids_ref, comb_ref, wg_ref, wu_ref, wd_ref,
    first_ref, second_ref, gg_ref, gu_ref, gd_ref,
    wgu, wd, xs, ws, gs, hs, g_far, h_far, send, back, got, dy_next,
    pre, hg, key, key_t, comb_t, h_t, stage_gu, stage_d,
    ssem, rsem, wsem, pair_send, pair_recv, y_send, y_recv, osem,
):
    section = lax.axis_index("section")
    place = lax.axis_index("expert")
    at_x, at_z, core = place // (2 * RING), (place // 2) % RING, place % 2

    def chip(slot, sign):
        dx, dz = slot // RING, slot % RING
        if sign < 0:
            dx, dz = (RING - dx) % RING, (RING - dz) % RING
        where = ((at_x + dx) % RING) * RING + (at_z + dz) % RING
        return (section, where * 2 + core)

    partner = (section, place + 1 - 2 * core)
    before = ((section + RING - 1) % RING, place)
    after = ((section + 1) % RING, place)

    barrier = pltpu.get_barrier_semaphore()
    for slot in range(1, PEERS):
        pl.semaphore_signal(barrier, inc=1, device_id=chip(slot, 1), device_id_type=MESH)
    pl.semaphore_signal(barrier, inc=1, device_id=partner, device_id_type=MESH)
    pl.semaphore_signal(barrier, inc=1, device_id=after, device_id_type=MESH)

    own = [
        pltpu.make_async_copy(wg_ref.at[0, 0], wgu.at[0, :, pl.ds(0, FF)], wsem.at[0]),
        pltpu.make_async_copy(wu_ref.at[0, 0], wgu.at[0, :, pl.ds(FF, FF)], wsem.at[1]),
        pltpu.make_async_copy(wd_ref.at[0, 0], wd.at[pl.ds(0, FF), :], wsem.at[2]),
    ]
    for copy in own:
        copy.start()

    def tables(m):
        ids = ids_ref[0, m]
        ids = jnp.concatenate([ids, ids], axis=0)
        weights = comb_ref[0, m].astype(F32)
        weights = jnp.concatenate([weights, weights], axis=0)
        lane = iota((2 * TOK, ALL), 1)
        row = iota((2 * TOK, ALL), 0)
        slot, c = lane // ROWS, lane % ROWS
        expert = ((at_x + slot // RING) % RING) * RING + (at_z + slot % RING) % RING
        named = jnp.zeros((2 * TOK, ALL), F32)
        combined = jnp.zeros((2 * TOK, ALL), F32)
        for k in range(3):
            hit = ids[:, k : k + 1] == expert
            named = jnp.where(hit, 1.0, named)
            combined = jnp.where(hit, weights[:, k : k + 1], combined)
        r2, c2 = iota((2 * TOK, 2 * TOK), 0), iota((2 * TOK, 2 * TOK), 1)
        earlier = (c2 < r2 % TOK).astype(F32).astype(BF16)
        rank = mm(earlier, named.astype(BF16))
        top = row < TOK
        base = jnp.where(top, c, 7 * (c - CAP)).astype(F32)
        fits = jnp.logical_and(named > 0.5, top == (c < CAP))
        value = jnp.where(fits, rank - base, -100.0)
        key[m] = value
        key_t[m] = value.T
        comb_t[m] = combined.T

    def payload(m, source, scaled, buf, rows_ref, base):
        def body(g, carry):
            data = jnp.concatenate([source[:, cols(g)], source[:, pl.ds(WIDE, GROUP)]], axis=0)
            lane = iota((ALL, 2 * TOK), 1)
            wanted = jnp.where(lane < TOK, 0, g).astype(F32)
            table = jnp.where(key_t[m] == wanted, comb_t[m] if scaled else 1.0, 0.0)
            value = mm(table.astype(BF16), data).astype(BF16)
            send[buf, :, cols(g)] = value
            rows_ref[pl.ds(base, ROWS), cols(g)] = value[:ROWS]
            return carry

        lax.fori_loop(0, FULL, body, 0)

    def dispatch(phase, buf, rows_ref, base, slots):
        for slot in slots:
            pltpu.make_async_remote_copy(
                src_ref=send.at[buf, pl.ds(slot * ROWS, ROWS), :],
                dst_ref=rows_ref.at[pl.ds(base + slot * ROWS, ROWS), pl.ds(0, WIDE)],
                send_sem=ssem.at[phase],
                recv_sem=rsem.at[phase],
                device_id=chip(slot, 1),
                device_id_type=MESH,
            ).start()

    def sent(phase, ref):
        part = ref.at[pl.ds(ROWS, ALL - ROWS), :]
        pltpu.make_async_copy(part, part, ssem.at[phase]).wait()

    def arrived(phase, ref, base):
        part = ref.at[pl.ds(base + ROWS, ALL - ROWS), pl.ds(0, WIDE)]
        pltpu.make_async_copy(part, part, rsem.at[phase]).wait()

    def unfold(ref, base):
        total = jnp.zeros((ALL, GROUP), F32)
        for g in range(FULL):
            total = total + mm(
                spread(g, False), ref[pl.ds(base, ALL), pl.ds(g * GROUP, GROUP)]
            )
        ref[pl.ds(base, ALL), pl.ds(WIDE, GROUP)] = total.astype(BF16)

    def to_partner(n, src, dst):
        return pltpu.make_async_remote_copy(
            src_ref=src, dst_ref=dst, send_sem=pair_send.at[n], recv_sem=pair_recv.at[n],
            device_id=partner, device_id_type=MESH,
        )

    def rows_of(part):
        return pl.ds(part * ALL, ALL)

    def forward(m):
        base = 2 * m * ALL

        def body(n, carry):
            half, tile = n // 3, pl.ds(pl.multiple_of((n % 3) * 256, 256), 256)
            pre[half, :, tile] = mm(xs[pl.ds(base, ALL), :], wgu[half, :, tile])
            return carry

        lax.fori_loop(0, 6, body, 0)

    def hidden_terms(m):
        base = 2 * m * ALL

        def body(n, carry):
            tile = pl.ds(pl.multiple_of(n * 256, 256), 256)
            hg[:, tile] = mm_t(ws[pl.ds(base, ALL), :], wd[tile, :])
            return carry

        lax.fori_loop(0, 3, body, 0)
        real = iota((ALL, FF), 0) % ROWS < CAP
        for half in range(2):
            gate, up = pre[half, :, :FF], pre[half, :, FF:]
            grad = hg[:, half * FF : (half + 1) * FF]
            sig = jax.nn.sigmoid(gate)
            active = gate * sig
            hidden = jnp.where(real, active * up, 0.0).astype(BF16)
            gate_rows = grad * up * sig * (1.0 + gate * (1.0 - sig))
            gate_rows = jnp.where(real, gate_rows, 0.0).astype(BF16)
            up_rows = jnp.where(real, grad * active, 0.0).astype(BF16)
            if half == 0:
                gs[pl.ds(base, ALL), :FF] = gate_rows
                gs[pl.ds(base, ALL), FF:] = up_rows
                hs[pl.ds(base, ALL), :] = hidden
            else:
                g_far[m, :, :FF] = gate_rows
                g_far[m, :, FF:] = up_rows
                h_far[m] = hidden

    def partial(m, g):
        base = 2 * m * ALL
        near = mm_t(gs[pl.ds(base, ALL), :], wgu[0, cols(g), :])
        return near + mm_t(g_far[m], wgu[1, cols(g), :])

    def partials(m):
        folded = partial(m, FULL).astype(BF16)

        def body(g, carry):
            value = (partial(m, g) + mm(spread(g, True), folded)).astype(BF16)
            back[:, cols(g)] = value
            got[pl.ds(0, ROWS), cols(g)] = value[:ROWS]
            return carry

        lax.fori_loop(0, FULL, body, 0)

    def give_back(phase):
        for slot in ORDER:
            pltpu.make_async_remote_copy(
                src_ref=back.at[pl.ds(slot * ROWS, ROWS), :],
                dst_ref=got.at[pl.ds(slot * ROWS, ROWS), :],
                send_sem=ssem.at[phase],
                recv_sem=rsem.at[phase],
                device_id=chip(slot, -1),
                device_id_type=MESH,
            ).start()

    def combine(m, grads, out):
        picked = jnp.where(key[m, :TOK] == 0.0, 1.0, 0.0).astype(BF16)

        def body(g, total):
            block = got[:, cols(g)]
            out[0, :, cols(g)] = (grads[:, cols(g)].astype(F32) + mm(picked, block)).astype(BF16)
            folded = jnp.where(key[m, TOK:] == g.astype(F32), 1.0, 0.0).astype(BF16)
            return total + mm(folded, block)

        total = lax.fori_loop(0, FULL, body, jnp.zeros((TOK, GROUP), F32))
        tail = pl.ds(WIDE, GROUP)
        out[0, :, tail] = (grads[:, tail].astype(F32) + total).astype(BF16)

    tables(0)
    payload(0, x_ref.at[0, 0], False, 0, xs, 0)
    pl.semaphore_wait(barrier, PEERS + 1)
    dispatch(0, 0, xs, 0, ORDER)
    far = [
        to_partner(0, wg_ref.at[0, 0], wgu.at[1, :, pl.ds(0, FF)]),
        to_partner(1, wu_ref.at[0, 0], wgu.at[1, :, pl.ds(FF, FF)]),
        to_partner(2, wd_ref.at[0, 0], wd.at[pl.ds(FF, FF), :]),
    ]
    for copy in far:
        copy.start()
    payload(0, dy_ref.at[0], True, 1, ws, 0)
    dispatch(1, 1, ws, 0, ORDER)
    tables(1)
    payload(1, x_ref.at[0, 1], False, 2, xs, 2 * ALL)
    dispatch(3, 2, xs, 2 * ALL, ORDER[:5])

    for copy in own:
        copy.wait()
    for copy in far:
        copy.wait()
    arrived(0, xs, 0)
    unfold(xs, 0)
    pair = [to_partner(3, xs.at[rows_of(0), :], xs.at[rows_of(1), :])]
    pair[-1].start()
    forward(0)
    arrived(1, ws, 0)
    unfold(ws, 0)
    pair.append(to_partner(4, ws.at[rows_of(0), :], ws.at[rows_of(1), :]))
    pair[-1].start()
    hidden_terms(0)
    partials(0)
    give_back(2)
    dispatch(3, 2, xs, 2 * ALL, ORDER[5:])
    pair.append(to_partner(5, g_far.at[0], gs.at[rows_of(1), :]))
    pair[-1].start()
    pair.append(to_partner(6, h_far.at[0], hs.at[rows_of(1), :]))
    pair[-1].start()
    sent(0, send.at[0])

    arrived(2, got, 0)
    combine(0, dy_ref.at[0], first_ref)
    relay = pltpu.make_async_remote_copy(
        src_ref=first_ref.at[0], dst_ref=dy_next, send_sem=y_send, recv_sem=y_recv,
        device_id=before, device_id_type=MESH,
    )
    relay.start()
    relay.wait()

    @pl.when(section == RING - 1)
    def _():
        dy_next[...] = last_ref[...]

    payload(1, dy_next, True, 0, ws, 2 * ALL)
    dispatch(4, 0, ws, 2 * ALL, ORDER)
    sent(2, back)
    arrived(3, xs, 2 * ALL)
    unfold(xs, 2 * ALL)
    pair.append(to_partner(7, xs.at[rows_of(2), :], xs.at[rows_of(3), :]))
    pair[-1].start()
    forward(1)
    arrived(4, ws, 2 * ALL)
    unfold(ws, 2 * ALL)
    pair.append(to_partner(8, ws.at[rows_of(2), :], ws.at[rows_of(3), :]))
    pair[-1].start()
    hidden_terms(1)
    pair.append(to_partner(9, g_far.at[1], gs.at[rows_of(3), :]))
    pair[-1].start()
    pair.append(to_partner(10, h_far.at[1], hs.at[rows_of(3), :]))
    pair[-1].start()
    partials(1)
    give_back(5)

    for copy in pair:
        copy.wait()
    h_t[...] = hs[...].astype(F32).T.astype(BF16)

    def stores(d):
        slot = d % 2
        rows = cols(d)
        return [
            pltpu.make_async_copy(
                stage_gu.at[slot, :, pl.ds(0, FF)], gg_ref.at[0, 0, rows, :], osem.at[slot, 0]
            ),
            pltpu.make_async_copy(
                stage_gu.at[slot, :, pl.ds(FF, FF)], gu_ref.at[0, 0, rows, :], osem.at[slot, 1]
            ),
            pltpu.make_async_copy(stage_d.at[slot], gd_ref.at[0, 0, :, rows], osem.at[slot, 2]),
        ]

    def weight_body(d, carry):
        @pl.when(d >= 2)
        def _():
            for copy in stores(d - 2):
                copy.wait()

        slot = d % 2
        value = lax.dot_general(xs[:, cols(d)], gs[...], DOWN, preferred_element_type=F32)
        stage_gu[slot] = value.astype(BF16)
        stage_d[slot] = mm(h_t[...], ws[:, cols(d)]).astype(BF16)
        for copy in stores(d):
            copy.start()
        return carry

    lax.fori_loop(0, D // GROUP, weight_body, 0)

    arrived(5, got, 0)
    combine(1, dy_next, second_ref)
    for d in range(D // GROUP - 2, D // GROUP):
        for copy in stores(d):
            copy.wait()
    sent(1, send.at[1])
    sent(3, send.at[2])
    sent(4, send.at[0])
    sent(5, back)


def local(saved_inputs, arriving, last_grad, expert_ids, combine, w_gate, w_up, w_down):
    vmem = pl.BlockSpec(memory_space=pltpu.VMEM)
    hbm = pl.BlockSpec(memory_space=pl.ANY)
    grads = jax.ShapeDtypeStruct(arriving.shape, BF16)
    dma = pltpu.SemaphoreType.DMA
    return pl.pallas_call(
        kernel,
        out_shape=(
            grads,
            grads,
            jax.ShapeDtypeStruct(w_gate.shape, BF16),
            jax.ShapeDtypeStruct(w_up.shape, BF16),
            jax.ShapeDtypeStruct(w_down.shape, BF16),
        ),
        in_specs=[vmem] * 5 + [hbm] * 3,
        out_specs=(vmem, vmem, hbm, hbm, hbm),
        scratch_shapes=[
            pltpu.VMEM((2, D, 2 * FF), BF16),
            pltpu.VMEM((2 * FF, D), BF16),
            pltpu.VMEM((4 * ALL, D), BF16),
            pltpu.VMEM((4 * ALL, D), BF16),
            pltpu.VMEM((4 * ALL, 2 * FF), BF16),
            pltpu.VMEM((4 * ALL, FF), BF16),
            pltpu.VMEM((2, ALL, 2 * FF), BF16),
            pltpu.VMEM((2, ALL, FF), BF16),
            pltpu.VMEM((3, ALL, WIDE), BF16),
            pltpu.VMEM((ALL, WIDE), BF16),
            pltpu.VMEM((ALL, WIDE), BF16),
            pltpu.VMEM((TOK, D), BF16),
            pltpu.VMEM((2, ALL, 2 * FF), F32),
            pltpu.VMEM((ALL, 2 * FF), F32),
            pltpu.VMEM((2, 2 * TOK, ALL), F32),
            pltpu.VMEM((2, ALL, 2 * TOK), F32),
            pltpu.VMEM((2, ALL, 2 * TOK), F32),
            pltpu.VMEM((FF, 4 * ALL), BF16),
            pltpu.VMEM((2, GROUP, 2 * FF), BF16),
            pltpu.VMEM((2, FF, GROUP), BF16),
            dma((6,)),
            dma((6,)),
            dma((3,)),
            dma((11,)),
            dma((11,)),
            dma,
            dma,
            dma((2, 3)),
        ],
        compiler_params=pltpu.CompilerParams(
            collective_id=0, has_side_effects=True, vmem_limit_bytes=63 << 20
        ),
        name="relay_backward",
    )(saved_inputs, arriving, last_grad, expert_ids, combine, w_gate, w_up, w_down)


def solution(mesh):
    return jax.shard_map(
        local,
        mesh=mesh,
        in_specs=(
            P("section", None, "expert", None),
            P("section", "expert", None),
            P("expert", None),
            P("section", None, "expert", None),
            P("section", None, "expert", None),
            P("section", "expert", None, None),
            P("section", "expert", None, None),
            P("section", "expert", None, None),
        ),
        out_specs=(
            P("section", "expert", None),
            P("section", "expert", None),
            P("section", "expert", None, None),
            P("section", "expert", None, None),
            P("section", "expert", None, None),
        ),
        check_vma=False,
    )
```

time: 672 us -> 187 us (0.28)
  the two profiles are of different devices: /device:TPU:52 before, /device:TPU:16 now
where the time goes in v1:
time: 187 us; the launch traced here: 186 us
  Pallas kernels  170 us (91%)
  local copies, waits for them, and re-layouts  15.3 us (8%)
    pallas_call x1, Pallas kernels, local(): pl.pallas_call(kernel, out_shape=(grads, grads, jax.ShapeDtypeStruct(w_ga...  170 us
    unnamed x11, local copies, waits for them, and re-layouts  15.3 us

profile of v1, /device:TPU:16, one launch (start us, length us, event | category | flops | bytes accessed | tf_op | source)
XLA Modules:
  0.0 186.2 jit_solution(3073652256027547819)
XLA Ops:
  0.6 1.4 copy.14.comb_ref
  2.0 1.4 copy.13.ids_ref
  3.4 170.3 %relay_backward.1 = (bf16[1,64,4096]{2,1,0:T(8,128)(2,1)}, bf16[1,64,4096]{2,1,0:T(8,128)(2,1)}, bf16[1,1,4096,384]{3,2,1,0:T(8,128)(2,1)}, bf16[1,1,4096,384]{3,2,1,0:T(8,128)(2,1)}, bf16[1,1,384,4096]{3,2,1,0:T(8,128)(2,1)}) custom-call(bf16[1,2,64,4096]{3,2,1,0:T(8,128)(2,1)} %x_ref.1, bf16[1,64,4096]{2,1,0:T(8,128)(2,1)} %dy_ref.1, ...), custom_call_target="tpu_custom_call" | custom-call | tf_op jit(solution)/shard_map/relay_backward/pallas_call | solution.py:371
  173.8 1.9 %copy.20 = bf16[1,64,4096]{2,1,0:T(8,128)(2,1)} copy(bf16[1,64,4096]{2,1,0:T(8,128)(2,1)} %get-tuple-element.10) | data formatting | bytes 1048576
  175.7 1.9 %copy.21 = bf16[1,64,4096]{2,1,0:T(8,128)(2,1)} copy(bf16[1,64,4096]{2,1,0:T(8,128)(2,1)} %get-tuple-element.11) | data formatting | bytes 1048576
  177.5 0.0 copy-start.1
  177.5 4.0 %copy.22 = bf16[1,1,4096,384]{3,2,1,0:T(8,128)(2,1)} copy(bf16[1,1,4096,384]{3,2,1,0:T(8,128)(2,1)} %get-tuple-element.12) | data formatting | bytes 6291456
  181.5 0.0 copy-done.1
  181.5 0.0 copy-start
  181.5 1.7 copy.23
  183.2 1.4 copy-done
  184.6 1.7 copy.24
Async XLA Ops:
  177.5 4.0 %copy-start.1 = (bf16[1,1,4096,384]{3,2,1,0:T(8,128)(2,1)S(1)}, bf16[1,1,4096,384]{3,2,1,0:T(8,128)(2,1)}, u32[]{:S(2)}) copy-start(bf16[1,1,4096,384]{3,2,1,0:T(8,128)(2,1)} %get-tuple-element.13) | copy-start | bytes 9437188
  181.5 3.0 %copy-start = (bf16[1,1,384,4096]{3,2,1,0:T(8,128)(2,1)S(1)}, bf16[1,1,384,4096]{3,2,1,0:T(8,128)(2,1)}, u32[]{:S(2)}) copy-start(bf16[1,1,384,4096]{3,2,1,0:T(8,128)(2,1)} %get-tuple-element.14) | copy-start | bytes 9437188

commit v2 on v1

--- a/solution.py
+++ b/solution.py
@@ -21,13 +21,12 @@
 FF = 384
 ALL = PEERS * ROWS
 
-ORDER = tuple(
-    (dx % RING) * RING + dz % RING
-    for dx, dz in (
-        (2, 2), (1, 0), (-1, 0), (2, 1), (0, -1), (1, 2), (0, 1), (2, -1),
-        (1, 1), (-1, 2), (-1, -1), (2, 0), (1, -1), (0, 2), (-1, 1),
-    )
+STEPS = (
+    (0, 0), (2, 2), (1, 0), (-1, 2), (0, 1), (2, 1), (0, -1), (2, -1),
+    (1, 2), (-1, 0), (1, 1), (0, 2), (-1, -1), (2, 0), (1, -1), (-1, 1),
 )
+EARLY, LATE = range(1, 8), range(8, 16)
+HALF = ALL // 2
 
 ACROSS = (((1,), (1,)), ((), ()))
 DOWN = (((0,), (0,)), ((), ()))
@@ -45,8 +44,8 @@
     return lax.broadcasted_iota(jnp.int32, shape, axis)
 
 
-def spread(group, transposed):
-    to, come = iota((ALL, ALL), int(transposed)), iota((ALL, ALL), int(not transposed))
+def spread(group, transposed, count):
+    to, come = iota((count, count), int(transposed)), iota((count, count), int(not transposed))
     slot = to % ROWS
     late = (slot >= 7).astype(jnp.int32)
     hit = jnp.logical_and(come == to - slot + CAP + late, slot - 7 * late == group)
@@ -68,12 +67,12 @@
     place = lax.axis_index("expert")
     at_x, at_z, core = place // (2 * RING), (place // 2) % RING, place % 2
 
+    def expert_at(slot, sign):
+        dx, dz = (sign * step % RING for step in STEPS[slot])
+        return ((at_x + dx) % RING) * RING + (at_z + dz) % RING
+
     def chip(slot, sign):
-        dx, dz = slot // RING, slot % RING
-        if sign < 0:
-            dx, dz = (RING - dx) % RING, (RING - dz) % RING
-        where = ((at_x + dx) % RING) * RING + (at_z + dz) % RING
-        return (section, where * 2 + core)
+        return (section, expert_at(slot, sign) * 2 + core)
 
     partner = (section, place + 1 - 2 * core)
     before = ((section + RING - 1) % RING, place)
@@ -94,30 +93,30 @@
         copy.start()
 
     def tables(m):
-        ids = ids_ref[0, m]
-        ids = jnp.concatenate([ids, ids], axis=0)
-        weights = comb_ref[0, m].astype(F32)
-        weights = jnp.concatenate([weights, weights], axis=0)
-        lane = iota((2 * TOK, ALL), 1)
-        row = iota((2 * TOK, ALL), 0)
-        slot, c = lane // ROWS, lane % ROWS
-        expert = ((at_x + slot // RING) % RING) * RING + (at_z + slot % RING) % RING
-        named = jnp.zeros((2 * TOK, ALL), F32)
-        combined = jnp.zeros((2 * TOK, ALL), F32)
+        shape = (ALL, 2 * TOK)
+        row, lane = iota(shape, 0), iota(shape, 1)
+        c = row % ROWS
+        expert = jnp.concatenate(
+            [jnp.full((ROWS, 2 * TOK), expert_at(slot, 1), jnp.int32) for slot in range(PEERS)], axis=0
+        )
+        named = jnp.zeros(shape, F32)
+        combined = jnp.zeros(shape, F32)
         for k in range(3):
-            hit = ids[:, k : k + 1] == expert
+            ids = ids_ref[0, k, m : m + 1, :]
+            weights = comb_ref[0, k, m : m + 1, :].astype(F32)
+            hit = jnp.concatenate([ids, ids], axis=1) == expert
             named = jnp.where(hit, 1.0, named)
-            combined = jnp.where(hit, weights[:, k : k + 1], combined)
+            combined = jnp.where(hit, jnp.concatenate([weights, weights], axis=1), combined)
         r2, c2 = iota((2 * TOK, 2 * TOK), 0), iota((2 * TOK, 2 * TOK), 1)
-        earlier = (c2 < r2 % TOK).astype(F32).astype(BF16)
-        rank = mm(earlier, named.astype(BF16))
-        top = row < TOK
+        earlier = (r2 < c2 % TOK).astype(F32).astype(BF16)
+        rank = mm(named.astype(BF16), earlier)
+        top = lane < TOK
         base = jnp.where(top, c, 7 * (c - CAP)).astype(F32)
         fits = jnp.logical_and(named > 0.5, top == (c < CAP))
         value = jnp.where(fits, rank - base, -100.0)
-        key[m] = value
-        key_t[m] = value.T
-        comb_t[m] = combined.T
+        key_t[m] = value
+        key[m] = value.T
+        comb_t[m] = combined
 
     def payload(m, source, scaled, buf, rows_ref, base):
         def body(g, carry):
@@ -143,21 +142,21 @@
                 device_id_type=MESH,
             ).start()
 
-    def sent(phase, ref):
-        part = ref.at[pl.ds(ROWS, ALL - ROWS), :]
+    def sent(phase, ref, lo=ROWS, hi=ALL):
+        part = ref.at[pl.ds(lo, hi - lo), :]
         pltpu.make_async_copy(part, part, ssem.at[phase]).wait()
 
-    def arrived(phase, ref, base):
-        part = ref.at[pl.ds(base + ROWS, ALL - ROWS), pl.ds(0, WIDE)]
+    def arrived(phase, ref, base, lo=ROWS, hi=ALL):
+        part = ref.at[pl.ds(base + lo, hi - lo), pl.ds(0, WIDE)]
         pltpu.make_async_copy(part, part, rsem.at[phase]).wait()
 
-    def unfold(ref, base):
-        total = jnp.zeros((ALL, GROUP), F32)
+    def unfold(ref, base, count):
+        total = jnp.zeros((count, GROUP), F32)
         for g in range(FULL):
             total = total + mm(
-                spread(g, False), ref[pl.ds(base, ALL), pl.ds(g * GROUP, GROUP)]
+                spread(g, False, count), ref[pl.ds(base, count), pl.ds(g * GROUP, GROUP)]
             )
-        ref[pl.ds(base, ALL), pl.ds(WIDE, GROUP)] = total.astype(BF16)
+        ref[pl.ds(base, count), pl.ds(WIDE, GROUP)] = total.astype(BF16)
 
     def to_partner(n, src, dst):
         return pltpu.make_async_remote_copy(
@@ -178,19 +177,20 @@
 
         lax.fori_loop(0, 6, body, 0)
 
-    def hidden_terms(m):
-        base = 2 * m * ALL
+    def hidden_terms(m, lo, count):
+        base = 2 * m * ALL + lo
 
         def body(n, carry):
             tile = pl.ds(pl.multiple_of(n * 256, 256), 256)
-            hg[:, tile] = mm_t(ws[pl.ds(base, ALL), :], wd[tile, :])
+            hg[pl.ds(lo, count), tile] = mm_t(ws[pl.ds(base, count), :], wd[tile, :])
             return carry
 
         lax.fori_loop(0, 3, body, 0)
-        real = iota((ALL, FF), 0) % ROWS < CAP
+        real = iota((count, FF), 0) % ROWS < CAP
+        part = pl.ds(lo, count)
         for half in range(2):
-            gate, up = pre[half, :, :FF], pre[half, :, FF:]
-            grad = hg[:, half * FF : (half + 1) * FF]
+            gate, up = pre[half, part, :FF], pre[half, part, FF:]
+            grad = hg[part, half * FF : (half + 1) * FF]
             sig = jax.nn.sigmoid(gate)
             active = gate * sig
             hidden = jnp.where(real, active * up, 0.0).astype(BF16)
@@ -198,32 +198,32 @@
             gate_rows = jnp.where(real, gate_rows, 0.0).astype(BF16)
             up_rows = jnp.where(real, grad * active, 0.0).astype(BF16)
             if half == 0:
-                gs[pl.ds(base, ALL), :FF] = gate_rows
-                gs[pl.ds(base, ALL), FF:] = up_rows
-                hs[pl.ds(base, ALL), :] = hidden
+                gs[pl.ds(base, count), :FF] = gate_rows
+                gs[pl.ds(base, count), FF:] = up_rows
+                hs[pl.ds(base, count), :] = hidden
             else:
-                g_far[m, :, :FF] = gate_rows
-                g_far[m, :, FF:] = up_rows
-                h_far[m] = hidden
-
-    def partial(m, g):
-        base = 2 * m * ALL
-        near = mm_t(gs[pl.ds(base, ALL), :], wgu[0, cols(g), :])
-        return near + mm_t(g_far[m], wgu[1, cols(g), :])
-
-    def partials(m):
-        folded = partial(m, FULL).astype(BF16)
+                g_far[m, part, :FF] = gate_rows
+                g_far[m, part, FF:] = up_rows
+                h_far[m, part, :] = hidden
+
+    def partials(m, lo, count):
+        def partial(g):
+            near = mm_t(gs[pl.ds(2 * m * ALL + lo, count), :], wgu[0, cols(g), :])
+            return near + mm_t(g_far[m, pl.ds(lo, count), :], wgu[1, cols(g), :])
+
+        folded = partial(FULL).astype(BF16)
 
         def body(g, carry):
-            value = (partial(m, g) + mm(spread(g, True), folded)).astype(BF16)
-            back[:, cols(g)] = value
-            got[pl.ds(0, ROWS), cols(g)] = value[:ROWS]
+            value = (partial(g) + mm(spread(g, True, count), folded)).astype(BF16)
+            back[pl.ds(lo, count), cols(g)] = value
+            if lo == 0:
+                got[pl.ds(0, ROWS), cols(g)] = value[:ROWS]
             return carry
 
         lax.fori_loop(0, FULL, body, 0)
 
-    def give_back(phase):
-        for slot in ORDER:
+    def give_back(phase, slots):
+        for slot in slots:
             pltpu.make_async_remote_copy(
                 src_ref=back.at[pl.ds(slot * ROWS, ROWS), :],
                 dst_ref=got.at[pl.ds(slot * ROWS, ROWS), :],
@@ -249,7 +249,7 @@
     tables(0)
     payload(0, x_ref.at[0, 0], False, 0, xs, 0)
     pl.semaphore_wait(barrier, PEERS + 1)
-    dispatch(0, 0, xs, 0, ORDER)
+    dispatch(0, 0, xs, 0, range(1, PEERS))
     far = [
         to_partner(0, wg_ref.at[0, 0], wgu.at[1, :, pl.ds(0, FF)]),
         to_partner(1, wu_ref.at[0, 0], wgu.at[1, :, pl.ds(FF, FF)]),
@@ -258,28 +258,27 @@
     for copy in far:
         copy.start()
     payload(0, dy_ref.at[0], True, 1, ws, 0)
-    dispatch(1, 1, ws, 0, ORDER)
+    dispatch(1, 1, ws, 0, range(1, PEERS))
     tables(1)
     payload(1, x_ref.at[0, 1], False, 2, xs, 2 * ALL)
-    dispatch(3, 2, xs, 2 * ALL, ORDER[:5])
 
     for copy in own:
         copy.wait()
     for copy in far:
         copy.wait()
     arrived(0, xs, 0)
-    unfold(xs, 0)
+    unfold(xs, 0, ALL)
     pair = [to_partner(3, xs.at[rows_of(0), :], xs.at[rows_of(1), :])]
     pair[-1].start()
     forward(0)
     arrived(1, ws, 0)
-    unfold(ws, 0)
+    dispatch(3, 2, xs, 2 * ALL, EARLY)
+    unfold(ws, 0, ALL)
     pair.append(to_partner(4, ws.at[rows_of(0), :], ws.at[rows_of(1), :]))
     pair[-1].start()
-    hidden_terms(0)
-    partials(0)
-    give_back(2)
-    dispatch(3, 2, xs, 2 * ALL, ORDER[5:])
+    hidden_terms(0, 0, ALL)
+    partials(0, 0, ALL)
+    give_back(2, range(1, PEERS))
     pair.append(to_partner(5, g_far.at[0], gs.at[rows_of(1), :]))
     pair[-1].start()
     pair.append(to_partner(6, h_far.at[0], hs.at[rows_of(1), :]))
@@ -287,6 +286,7 @@
     sent(0, send.at[0])
 
     arrived(2, got, 0)
+    dispatch(3, 2, xs, 2 * ALL, LATE)
     combine(0, dy_ref.at[0], first_ref)
     relay = pltpu.make_async_remote_copy(
         src_ref=first_ref.at[0], dst_ref=dy_next, send_sem=y_send, recv_sem=y_recv,
@@ -300,24 +300,30 @@
         dy_next[...] = last_ref[...]
 
     payload(1, dy_next, True, 0, ws, 2 * ALL)
-    dispatch(4, 0, ws, 2 * ALL, ORDER)
+    dispatch(4, 0, ws, 2 * ALL, EARLY)
+    dispatch(5, 0, ws, 2 * ALL, LATE)
     sent(2, back)
     arrived(3, xs, 2 * ALL)
-    unfold(xs, 2 * ALL)
+    unfold(xs, 2 * ALL, ALL)
     pair.append(to_partner(7, xs.at[rows_of(2), :], xs.at[rows_of(3), :]))
     pair[-1].start()
     forward(1)
-    arrived(4, ws, 2 * ALL)
-    unfold(ws, 2 * ALL)
+    arrived(4, ws, 2 * ALL, ROWS, HALF)
+    unfold(ws, 2 * ALL, HALF)
+    hidden_terms(1, 0, HALF)
+    partials(1, 0, HALF)
+    give_back(6, EARLY)
+    arrived(5, ws, 2 * ALL, HALF, ALL)
+    unfold(ws, 2 * ALL + HALF, HALF)
     pair.append(to_partner(8, ws.at[rows_of(2), :], ws.at[rows_of(3), :]))
     pair[-1].start()
-    hidden_terms(1)
+    hidden_terms(1, HALF, HALF)
     pair.append(to_partner(9, g_far.at[1], gs.at[rows_of(3), :]))
     pair[-1].start()
     pair.append(to_partner(10, h_far.at[1], hs.at[rows_of(3), :]))
     pair[-1].start()
-    partials(1)
-    give_back(5)
+    partials(1, HALF, HALF)
+    give_back(6, LATE)
 
     for copy in pair:
         copy.wait()
@@ -352,15 +358,38 @@
 
     lax.fori_loop(0, D // GROUP, weight_body, 0)
 
-    arrived(5, got, 0)
+    arrived(6, got, 0)
     combine(1, dy_next, second_ref)
     for d in range(D // GROUP - 2, D // GROUP):
         for copy in stores(d):
             copy.wait()
     sent(1, send.at[1])
     sent(3, send.at[2])
-    sent(4, send.at[0])
-    sent(5, back)
+    sent(4, send.at[0], ROWS, HALF)
+    sent(5, send.at[0], HALF, ALL)
+    sent(6, back)
+
+
+def place(*refs):
+    count = len(refs) // 3
+    sources, results, held = refs[:count], refs[count : 2 * count], refs[2 * count : 3 * count]
+    come, go = refs[3 * count :]
+    reads, writes = [], []
+    for source, result, buffer in zip(sources, results, held):
+        parts = 4 if source.size > 1 << 20 else 1
+        for p in range(parts):
+            size = source.shape[-2] // parts
+            rows = (0,) * (len(source.shape) - 2) + (pl.ds(p * size, size),)
+            n = len(reads)
+            reads.append(pltpu.make_async_copy(source.at[rows], buffer.at[rows], come.at[n]))
+            writes.append(pltpu.make_async_copy(buffer.at[rows], result.at[rows], go.at[n]))
+    for read in reads:
+        read.start()
+    for read, write in zip(reads, writes):
+        read.wait()
+        write.start()
+    for write in writes:
+        write.wait()
 
 
 def local(saved_inputs, arriving, last_grad, expert_ids, combine, w_gate, w_up, w_down):
@@ -368,7 +397,7 @@
     hbm = pl.BlockSpec(memory_space=pl.ANY)
     grads = jax.ShapeDtypeStruct(arriving.shape, BF16)
     dma = pltpu.SemaphoreType.DMA
-    return pl.pallas_call(
+    results = pl.pallas_call(
         kernel,
         out_shape=(
             grads,
@@ -400,8 +429,8 @@
             pltpu.VMEM((FF, 4 * ALL), BF16),
             pltpu.VMEM((2, GROUP, 2 * FF), BF16),
             pltpu.VMEM((2, FF, GROUP), BF16),
-            dma((6,)),
-            dma((6,)),
+            dma((7,)),
+            dma((7,)),
             dma((3,)),
             dma((11,)),
             dma((11,)),
@@ -413,7 +442,19 @@
             collective_id=0, has_side_effects=True, vmem_limit_bytes=63 << 20
         ),
         name="relay_backward",
-    )(saved_inputs, arriving, last_grad, expert_ids, combine, w_gate, w_up, w_down)
+    )(
+        saved_inputs, arriving, last_grad, expert_ids.transpose(0, 3, 1, 2),
+        combine.transpose(0, 3, 1, 2), w_gate, w_up, w_down,
+    )
+    return pl.pallas_call(
+        place,
+        out_shape=tuple(jax.ShapeDtypeStruct(r.shape, r.dtype) for r in results),
+        in_specs=[hbm] * 5,
+        out_specs=(hbm,) * 5,
+        scratch_shapes=[pltpu.VMEM(r.shape, r.dtype) for r in results] + [dma((14,)), dma((14,))],
+        compiler_params=pltpu.CompilerParams(vmem_limit_bytes=63 << 20),
+        name="place",
+    )(*results)
 
 
 def solution(mesh):

time: 187 us -> 164 us (0.88)
  local copies, waits for them, and re-layouts: 15.3 us -> 0 us
  Pallas kernels: 170 us -> 162 us
    pallas_call x1, Pallas kernels: 170 us -> 154 us  [local(): pl.pallas_call(kernel, out_shape=(grads, grads, jax.ShapeDtypeStruct(w_ga...]
    unnamed x11 -> x0, local copies, waits for them, and re-layouts: 15.3 us -> none
    pallas_call x0 -> x1, Pallas kernels: none -> 7.96 us  [local(): pl.pallas_call(place, out_shape=tuple((jax.ShapeDtypeStruct(r.shape, r.dt...]
where the time goes in v2:
time: 164 us; the launch traced here: 163 us
  Pallas kernels  162 us (99%)
    pallas_call x1, Pallas kernels, local(): pl.pallas_call(kernel, out_shape=(grads, grads, jax.ShapeDtypeStruct(w_ga...  154 us
    pallas_call x1, Pallas kernels, local(): pl.pallas_call(place, out_shape=tuple((jax.ShapeDtypeStruct(r.shape, r.dt...  7.96 us

profile of v2, /device:TPU:16, one launch (start us, length us, event | category | flops | bytes accessed | tf_op | source)
XLA Modules:
  0.0 162.6 jit_solution(2106927875644596089)
XLA Ops:
  0.6 154.0 %relay_backward.1 = (bf16[1,64,4096]{2,1,0:T(8,128)(2,1)}, bf16[1,64,4096]{2,1,0:T(8,128)(2,1)}, bf16[1,1,4096,384]{3,2,1,0:T(8,128)(2,1)}, bf16[1,1,4096,384]{3,2,1,0:T(8,128)(2,1)}, bf16[1,1,384,4096]{3,2,1,0:T(8,128)(2,1)}) custom-call(bf16[1,2,64,4096]{3,2,1,0:T(8,128)(2,1)} %x_ref.1, bf16[1,64,4096]{2,1,0:T(8,128)(2,1)} %dy_ref.1, ...), custom_call_target="tpu_custom_call" | custom-call | tf_op jit(solution)/shard_map/relay_backward/pallas_call | solution.py:400
  154.7 8.0 %place.1 = (bf16[1,64,4096]{2,1,0:T(8,128)(2,1)}, bf16[1,64,4096]{2,1,0:T(8,128)(2,1)}, bf16[1,1,4096,384]{3,2,1,0:T(8,128)(2,1)}, bf16[1,1,4096,384]{3,2,1,0:T(8,128)(2,1)}, bf16[1,1,384,4096]{3,2,1,0:T(8,128)(2,1)}) custom-call(bf16[1,64,4096]{2,1,0:T(8,128)(2,1)} %get-tuple-element.10.refs_0_, bf16[1,64,4096]{2,1,0:T(8,128)(2,1)} %get-tuple-element.11.refs_1_, ...), custom_call_target="tpu_custom_call" | custom-call | tf_op jit(solution)/shard_map/place/pallas_call | solution.py:449

commit v3 on v2

v3 whole, which is shorter than its diff:
```python
import jax
import jax.numpy as jnp
from jax import lax
from jax.experimental import pallas as pl
from jax.experimental.pallas import tpu as pltpu
from jax.sharding import PartitionSpec as P

MESH = pl.DeviceIdType.MESH
F32 = jnp.float32
BF16 = jnp.bfloat16

RING = 4
PEERS = RING * RING
ROWS = 16
CAP = 14
GROUP = 256
FULL = 7
WIDE = FULL * GROUP
D = 4096
SIDE = D // 2
BOTH = (0, 1)
TOK = 64
FF = 384
ALL = PEERS * ROWS

STEPS = (
    (0, 0), (2, 2), (1, 0), (-1, 2), (0, 1), (2, 1), (0, -1), (2, -1),
    (1, 2), (-1, 0), (1, 1), (0, 2), (-1, -1), (2, 0), (1, -1), (-1, 1),
)
EARLY, LATE, OTHERS = range(1, 8), range(8, 16), range(1, 16)
HALF = ALL // 2

ACROSS = (((1,), (1,)), ((), ()))
DOWN = (((0,), (0,)), ((), ()))


def mm(a, b):
    return jnp.dot(a, b, preferred_element_type=F32)


def mm_t(a, b):
    return lax.dot_general(a, b, ACROSS, preferred_element_type=F32)


def iota(shape, axis):
    return lax.broadcasted_iota(jnp.int32, shape, axis)


def spread(group, transposed, count):
    to, come = iota((count, count), int(transposed)), iota((count, count), int(not transposed))
    slot = to % ROWS
    late = (slot >= 7).astype(jnp.int32)
    hit = jnp.logical_and(come == to - slot + CAP + late, slot - 7 * late == group)
    return hit.astype(F32).astype(BF16)


def cols(half, group, count=1):
    return pl.ds(pl.multiple_of(half * SIDE + group * GROUP, GROUP), count * GROUP)


def sent_cols(half, group, count=1):
    return pl.ds(pl.multiple_of(half * WIDE + group * GROUP, GROUP), count * GROUP)


def tile(n, size):
    return pl.ds(pl.multiple_of(n * size, size), size)


def kernel(
    x_ref, dy_ref, last_ref, ids_ref, comb_ref, wg_ref, wu_ref, wd_ref,
    first_ref, second_ref, gg_ref, gu_ref, gd_ref,
    wgu, wd, xs, ws, gs, hs, g_far, h_far, send, back, got, dy_next,
    pre, hg, key, key_t, comb_t, h_t,
    ssem, rsem, wsem, pair_send, pair_recv, y_send, y_recv,
):
    section = lax.axis_index("section")
    place = lax.axis_index("expert")
    at_x, at_z, core = place // (2 * RING), (place // 2) % RING, place % 2

    def expert_at(slot, sign):
        dx, dz = (sign * step % RING for step in STEPS[slot])
        return ((at_x + dx) % RING) * RING + (at_z + dz) % RING

    def chip(slot, sign):
        return (section, expert_at(slot, sign) * 2 + core)

    partner = (section, place + 1 - 2 * core)
    before = ((section + RING - 1) % RING, place)
    after = ((section + 1) % RING, place)

    barrier = pltpu.get_barrier_semaphore()
    for slot in range(1, PEERS):
        pl.semaphore_signal(barrier, inc=1, device_id=chip(slot, 1), device_id_type=MESH)
    pl.semaphore_signal(barrier, inc=1, device_id=partner, device_id_type=MESH)
    pl.semaphore_signal(barrier, inc=1, device_id=after, device_id_type=MESH)

    own = [
        pltpu.make_async_copy(wg_ref.at[0, 0], gg_ref.at[0, 0], wsem.at[0]),
        pltpu.make_async_copy(wu_ref.at[0, 0], gu_ref.at[0, 0], wsem.at[1]),
        pltpu.make_async_copy(wd_ref.at[0, 0], gd_ref.at[0, 0], wsem.at[2]),
    ]
    for copy in own:
        copy.start()

    def tables(m):
        shape = (ALL, 2 * TOK)
        row, lane = iota(shape, 0), iota(shape, 1)
        c = row % ROWS
        expert = jnp.concatenate(
            [jnp.full((ROWS, 2 * TOK), expert_at(slot, 1), jnp.int32) for slot in range(PEERS)], axis=0
        )
        named = jnp.zeros(shape, F32)
        combined = jnp.zeros(shape, F32)
        for k in range(3):
            ids = ids_ref[0, k, m : m + 1, :]
            weights = comb_ref[0, k, m : m + 1, :].astype(F32)
            hit = jnp.concatenate([ids, ids], axis=1) == expert
            named = jnp.where(hit, 1.0, named)
            combined = jnp.where(hit, jnp.concatenate([weights, weights], axis=1), combined)
        r2, c2 = iota((2 * TOK, 2 * TOK), 0), iota((2 * TOK, 2 * TOK), 1)
        earlier = (r2 < c2 % TOK).astype(F32).astype(BF16)
        rank = mm(named.astype(BF16), earlier)
        top = lane < TOK
        base = jnp.where(top, c, 7 * (c - CAP)).astype(F32)
        fits = jnp.logical_and(named > 0.5, top == (c < CAP))
        value = jnp.where(fits, rank - base, -100.0)
        key_t[m] = value
        key[m] = value.T
        comb_t[m] = combined

    def payload(m, source, scaled, buf, rows_ref, base, halves=BOTH):
        def body(g, carry):
            data = jnp.concatenate(
                [
                    jnp.concatenate([source[:, cols(h, g)] for h in halves], axis=1),
                    jnp.concatenate([source[:, cols(h, FULL)] for h in halves], axis=1),
                ],
                axis=0,
            )
            lane = iota((ALL, 2 * TOK), 1)
            wanted = jnp.where(lane < TOK, 0, g).astype(F32)
            table = jnp.where(key_t[m] == wanted, comb_t[m] if scaled else 1.0, 0.0)
            value = mm(table.astype(BF16), data).astype(BF16)
            for n, h in enumerate(halves):
                piece = value[:, n * GROUP : (n + 1) * GROUP]
                send[buf, :, sent_cols(h, g)] = piece
                rows_ref[pl.ds(base, ROWS), cols(h, g)] = piece[:ROWS]
            return carry

        lax.fori_loop(0, FULL, body, 0)

    def dispatch(phase, buf, rows_ref, base, slots, halves=BOTH):
        for slot in slots:
            for h in halves:
                pltpu.make_async_remote_copy(
                    src_ref=send.at[buf, pl.ds(slot * ROWS, ROWS), sent_cols(h, 0, FULL)],
                    dst_ref=rows_ref.at[pl.ds(base + slot * ROWS, ROWS), cols(h, 0, FULL)],
                    send_sem=ssem.at[phase],
                    recv_sem=rsem.at[phase],
                    device_id=chip(slot, 1),
                    device_id_type=MESH,
                ).start()

    def settle(sem, slots, halves):
        part = back.at[pl.ds(slots[0] * ROWS, len(slots) * ROWS), pl.ds(0, len(halves) * WIDE)]
        pltpu.make_async_copy(part, part, sem).wait()

    def sent(phase, slots=OTHERS, halves=BOTH):
        settle(ssem.at[phase], slots, halves)

    def arrived(phase, slots=OTHERS, halves=BOTH):
        settle(rsem.at[phase], slots, halves)

    def unfold(ref, base, count, halves=BOTH):
        total = jnp.zeros((count, len(halves) * GROUP), F32)
        rows = pl.ds(base, count)
        for g in range(FULL):
            block = jnp.concatenate([ref[rows, cols(h, g)] for h in halves], axis=1)
            total = total + mm(spread(g, False, count), block)
        for n, h in enumerate(halves):
            ref[rows, cols(h, FULL)] = total[:, n * GROUP : (n + 1) * GROUP].astype(BF16)

    def to_partner(n, src, dst):
        return pltpu.make_async_remote_copy(
            src_ref=src, dst_ref=dst, send_sem=pair_send.at[n], recv_sem=pair_recv.at[n],
            device_id=partner, device_id_type=MESH,
        )

    def rows_of(part):
        return pl.ds(part * ALL, ALL)

    def forward(m):
        base = 2 * m * ALL

        def body(n, carry):
            pre[1, :, tile(n, 256)] = mm(xs[pl.ds(base, ALL), :], wgu[:, tile(n, 256)])
            return carry

        for n in range(3):
            lo, hi = n * 256, (n + 1) * 256
            pieces = [gg_ref[0, 0, :, lo : min(hi, FF)]] if lo < FF else []
            if hi > FF:
                pieces.append(gu_ref[0, 0, :, max(lo - FF, 0) : hi - FF])
            block = pieces[0] if len(pieces) == 1 else jnp.concatenate(pieces, axis=1)
            pre[0, :, lo:hi] = mm(xs[pl.ds(base, ALL), :], block)
        lax.fori_loop(0, 3, body, 0)

    def hidden_part(m, lo, count, h):
        rows, part = pl.ds(2 * m * ALL + lo, count), cols(h, 0, 8)

        for half, weights in ((0, gd_ref.at[0, 0]), (1, wd)):
            value = mm_t(weights[:, part], ws[rows, part]).T
            if h:
                value = value + hg[pl.ds(lo, count), half * FF : (half + 1) * FF]
            hg[pl.ds(lo, count), half * FF : (half + 1) * FF] = value

    def row_terms(m, lo, count):
        base = 2 * m * ALL + lo
        real = iota((count, FF), 0) % ROWS < CAP
        part = pl.ds(lo, count)
        for half in range(2):
            gate, up = pre[half, part, :FF], pre[half, part, FF:]
            grad = hg[part, half * FF : (half + 1) * FF]
            sig = jax.nn.sigmoid(gate)
            active = gate * sig
            hidden = jnp.where(real, active * up, 0.0).astype(BF16)
            gate_rows = grad * up * sig * (1.0 + gate * (1.0 - sig))
            gate_rows = jnp.where(real, gate_rows, 0.0).astype(BF16)
            up_rows = jnp.where(real, grad * active, 0.0).astype(BF16)
            if half == 0:
                gs[pl.ds(base, count), :FF] = gate_rows
                gs[pl.ds(base, count), FF:] = up_rows
                hs[pl.ds(base, count), :] = hidden
            else:
                g_far[m, part, :FF] = gate_rows
                g_far[m, part, FF:] = up_rows
                h_far[m, part, :] = hidden

    def partials(m, lo, count, h):
        def pair_of(n):
            part = cols(h, 2 * n, 2)
            own_part = jnp.concatenate([gg_ref[0, 0, part, :], gu_ref[0, 0, part, :]], axis=1)
            near = mm_t(gs[pl.ds(2 * m * ALL + lo, count), :], own_part)
            return near + mm_t(g_far[m, pl.ds(lo, count), :], wgu[part, :])

        def keep(g, value):
            value = (value + mm(spread(g, True, count), folded)).astype(BF16)
            back[pl.ds(lo, count), sent_cols(h, g)] = value
            if lo == 0:
                got[pl.ds(0, ROWS), sent_cols(h, g)] = value[:ROWS]

        last = pair_of(3)
        folded = last[:, GROUP:].astype(BF16)
        keep(6, last[:, :GROUP])

        def body(n, carry):
            value = pair_of(n)
            keep(2 * n, value[:, :GROUP])
            keep(2 * n + 1, value[:, GROUP:])
            return carry

        lax.fori_loop(0, 3, body, 0)

    def give_back(phase, slots, h):
        for slot in slots:
            pltpu.make_async_remote_copy(
                src_ref=back.at[pl.ds(slot * ROWS, ROWS), sent_cols(h, 0, FULL)],
                dst_ref=got.at[pl.ds(slot * ROWS, ROWS), sent_cols(h, 0, FULL)],
                send_sem=ssem.at[phase],
                recv_sem=rsem.at[phase],
                device_id=chip(slot, -1),
                device_id_type=MESH,
            ).start()

    def combine(m, grads, out, h):
        def body(g, total):
            wanted = jnp.where(iota((2 * TOK, ALL), 0) < TOK, 0, g).astype(F32)
            table = jnp.where(key[m] == wanted, 1.0, 0.0).astype(BF16)
            value = mm(table, got[:, sent_cols(h, g)])
            out[0, :, cols(h, g)] = (grads[:, cols(h, g)].astype(F32) + value[:TOK]).astype(BF16)
            return total + value[TOK:]

        total = lax.fori_loop(0, FULL, body, jnp.zeros((TOK, GROUP), F32))
        tail = cols(h, FULL)
        out[0, :, tail] = (grads[:, tail].astype(F32) + total).astype(BF16)

    tables(0)
    payload(0, x_ref.at[0, 0], False, 0, xs, 0)
    pl.semaphore_wait(barrier, PEERS + 1)
    dispatch(0, 0, xs, 0, OTHERS)
    far = [
        to_partner(0, wg_ref.at[0, 0], wgu.at[:, pl.ds(0, FF)]),
        to_partner(1, wu_ref.at[0, 0], wgu.at[:, pl.ds(FF, FF)]),
        to_partner(2, wd_ref.at[0, 0], wd),
    ]
    for copy in far:
        copy.start()
    payload(0, dy_ref.at[0], True, 1, ws, 0)
    dispatch(1, 1, ws, 0, OTHERS)
    tables(1)
    payload(1, x_ref.at[0, 1], False, 2, xs, 2 * ALL)

    for copy in own:
        copy.wait()
    for copy in far:
        copy.wait()
    arrived(0)
    unfold(xs, 0, ALL)
    pair = [to_partner(3, xs.at[rows_of(0), :], xs.at[rows_of(1), :])]
    pair[-1].start()
    forward(0)
    arrived(1)
    dispatch(4, 2, xs, 2 * ALL, EARLY)
    unfold(ws, 0, ALL)
    pair.append(to_partner(4, ws.at[rows_of(0), :], ws.at[rows_of(1), :]))
    pair[-1].start()
    for h in BOTH:
        hidden_part(0, 0, ALL, h)
    row_terms(0, 0, ALL)
    for h in BOTH:
        partials(0, 0, ALL, h)
        give_back(2 + h, OTHERS, h)
    pair.append(to_partner(5, g_far.at[0], gs.at[rows_of(1), :]))
    pair[-1].start()
    pair.append(to_partner(6, h_far.at[0], hs.at[rows_of(1), :]))
    pair[-1].start()
    sent(0)

    relays = [
        pltpu.make_async_remote_copy(
            src_ref=first_ref.at[0, :, cols(h, 0, 8)], dst_ref=dy_next.at[:, cols(h, 0, 8)],
            send_sem=y_send.at[h], recv_sem=y_recv.at[h], device_id=before, device_id_type=MESH,
        )
        for h in BOTH
    ]

    def take(h):
        relays[h].wait()

        @pl.when(section == RING - 1)
        def _():
            dy_next[:, cols(h, 0, 8)] = last_ref[:, cols(h, 0, 8)]

        payload(1, dy_next, True, 0, ws, 2 * ALL, (h,))

    arrived(2, OTHERS, (0,))
    combine(0, dy_ref.at[0], first_ref, 0)
    relays[0].start()
    take(0)
    dispatch(5, 0, ws, 2 * ALL, OTHERS, (0,))
    arrived(3, OTHERS, (1,))
    combine(0, dy_ref.at[0], first_ref, 1)
    relays[1].start()
    dispatch(4, 2, xs, 2 * ALL, LATE)
    take(1)
    dispatch(6, 0, ws, 2 * ALL, OTHERS, (1,))

    sent(2, OTHERS, (0,))
    sent(3, OTHERS, (1,))
    arrived(4)
    unfold(xs, 2 * ALL, ALL)
    pair.append(to_partner(7, xs.at[rows_of(2), :], xs.at[rows_of(3), :]))
    pair[-1].start()
    forward(1)
    arrived(5, OTHERS, (0,))
    unfold(ws, 2 * ALL, ALL, (0,))
    hidden_part(1, 0, ALL, 0)
    arrived(6, OTHERS, (1,))
    unfold(ws, 2 * ALL, ALL, (1,))
    pair.append(to_partner(8, ws.at[rows_of(2), :], ws.at[rows_of(3), :]))
    pair[-1].start()
    hidden_part(1, 0, ALL, 1)
    row_terms(1, 0, ALL)
    pair.append(to_partner(9, g_far.at[1], gs.at[rows_of(3), :]))
    pair[-1].start()
    pair.append(to_partner(10, h_far.at[1], hs.at[rows_of(3), :]))
    pair[-1].start()
    for h in BOTH:
        partials(1, 0, ALL, h)
        give_back(7 + h, OTHERS, h)

    for copy in pair:
        copy.wait()
    h_t[...] = hs[...].astype(F32).T.astype(BF16)

    def weight_body(d, carry):
        part = tile(d, 512)
        value = lax.dot_general(xs[:, part], gs[...], DOWN, preferred_element_type=F32)
        gg_ref[0, 0, part, :] = value[:, :FF].astype(BF16)
        gu_ref[0, 0, part, :] = value[:, FF:].astype(BF16)
        gd_ref[0, 0, :, part] = mm(h_t[...], ws[:, part]).astype(BF16)
        return carry

    lax.fori_loop(0, D // 512, weight_body, 0)

    for h in BOTH:
        arrived(7 + h, OTHERS, (h,))
        combine(1, dy_next, second_ref, h)
    sent(1)
    sent(4)
    sent(5, OTHERS, (0,))
    sent(6, OTHERS, (1,))
    for h in BOTH:
        sent(7 + h, OTHERS, (h,))


def place(*refs):
    count = (len(refs) - 1) // 2
    copies = []
    for source, result in zip(refs[:count], refs[count:-1]):
        parts = 4 if source.size > 1 << 20 else 1
        for p in range(parts):
            size = source.shape[-2] // parts
            rows = (0,) * (len(source.shape) - 2) + (pl.ds(p * size, size),)
            copies.append(pltpu.make_async_copy(source.at[rows], result.at[rows], refs[-1].at[len(copies)]))
    for copy in copies:
        copy.start()
    for copy in copies:
        copy.wait()


def local(saved_inputs, arriving, last_grad, expert_ids, combine, w_gate, w_up, w_down):
    vmem = pl.BlockSpec(memory_space=pltpu.VMEM)
    hbm = pl.BlockSpec(memory_space=pl.ANY)
    dma = pltpu.SemaphoreType.DMA
    results = pl.pallas_call(
        kernel,
        out_shape=tuple(pltpu.VMEM(a.shape, BF16) for a in (arriving, arriving, w_gate, w_up, w_down)),
        in_specs=[vmem] * 5 + [hbm] * 3,
        out_specs=(vmem,) * 5,
        scratch_shapes=[
            pltpu.VMEM((D, 2 * FF), BF16),
            pltpu.VMEM((FF, D), BF16),
            pltpu.VMEM((4 * ALL, D), BF16),
            pltpu.VMEM((4 * ALL, D), BF16),
            pltpu.VMEM((4 * ALL, 2 * FF), BF16),
            pltpu.VMEM((4 * ALL, FF), BF16),
            pltpu.VMEM((2, ALL, 2 * FF), BF16),
            pltpu.VMEM((2, ALL, FF), BF16),
            pltpu.VMEM((3, ALL, 2 * WIDE), BF16),
            pltpu.VMEM((ALL, 2 * WIDE), BF16),
            pltpu.VMEM((ALL, 2 * WIDE), BF16),
            pltpu.VMEM((TOK, D), BF16),
            pltpu.VMEM((2, ALL, 2 * FF), F32),
            pltpu.VMEM((ALL, 2 * FF), F32),
            pltpu.VMEM((2, 2 * TOK, ALL), F32),
            pltpu.VMEM((2, ALL, 2 * TOK), F32),
            pltpu.VMEM((2, ALL, 2 * TOK), F32),
            pltpu.VMEM((FF, 4 * ALL), BF16),
            dma((9,)),
            dma((9,)),
            dma((3,)),
            dma((11,)),
            dma((11,)),
            dma((2,)),
            dma((2,)),
        ],
        compiler_params=pltpu.CompilerParams(
            collective_id=0, has_side_effects=True, vmem_limit_bytes=50 << 20
        ),
        name="relay_backward",
    )(
        saved_inputs, arriving, last_grad, expert_ids.transpose(0, 3, 1, 2),
        combine.transpose(0, 3, 1, 2), w_gate, w_up, w_down,
    )
    return pl.pallas_call(
        place,
        out_shape=tuple(jax.ShapeDtypeStruct(r.shape, r.dtype) for r in results),
        in_specs=[vmem] * 5,
        out_specs=(hbm,) * 5,
        scratch_shapes=[dma((14,))],
        compiler_params=pltpu.CompilerParams(vmem_limit_bytes=1 << 20),
        name="place",
    )(*[pltpu.with_memory_space_constraint(r, pltpu.VMEM) for r in results])


def solution(mesh):
    return jax.shard_map(
        local,
        mesh=mesh,
        in_specs=(
            P("section", None, "expert", None),
            P("section", "expert", None),
            P("expert", None),
            P("section", None, "expert", None),
            P("section", None, "expert", None),
            P("section", "expert", None, None),
            P("section", "expert", None, None),
            P("section", "expert", None, None),
        ),
        out_specs=(
            P("section", "expert", None),
            P("section", "expert", None),
            P("section", "expert", None, None),
            P("section", "expert", None, None),
            P("section", "expert", None, None),
        ),
        check_vma=False,
    )
```

time: 164 us -> 148 us (0.902)
  Pallas kernels: 162 us -> 147 us
    pallas_call x1, Pallas kernels: 154 us -> 143 us  [local(): pl.pallas_call(kernel, out_shape=tuple((pltpu.VMEM(a.shape, BF16) for a i...]
    pallas_call x1, Pallas kernels: 7.96 us -> 4.04 us  [local(): pl.pallas_call(place, out_shape=tuple((jax.ShapeDtypeStruct(r.shape, r.dt...]
where the time goes in v3:
time: 148 us
  Pallas kernels  147 us (99%)
    pallas_call x1, Pallas kernels, local(): pl.pallas_call(kernel, out_shape=tuple((pltpu.VMEM(a.shape, BF16) for a i...  143 us
    pallas_call x1, Pallas kernels, local(): pl.pallas_call(place, out_shape=tuple((jax.ShapeDtypeStruct(r.shape, r.dt...  4.04 us

profile of v3, /device:TPU:16, one launch (start us, length us, event | category | flops | bytes accessed | tf_op | source)
XLA Modules:
  0.0 147.8 jit_solution(13383849397268895329)
XLA Ops:
  0.6 143.0 %relay_backward.1 = (bf16[1,64,4096]{2,1,0:T(8,128)(2,1)S(1)}, bf16[1,64,4096]{2,1,0:T(8,128)(2,1)S(1)}, bf16[1,1,4096,384]{3,2,1,0:T(8,128)(2,1)S(1)}, bf16[1,1...) custom-call(bf16[1,2,64,4096]{3,2,1,0:T(8,128)(2,1)} %x_ref.1, bf16[1,64,4096]{2,1,0:T(8,128)(2,1)} %dy_ref.1, ...), custom_call_target="tpu_custom_call" | custom-call | tf_op jit(solution)/shard_map/relay_backward/pallas_call | solution.py:426
  143.6 4.0 %place.1 = (bf16[1,64,4096]{2,1,0:T(8,128)(2,1)}, bf16[1,64,4096]{2,1,0:T(8,128)(2,1)}, bf16[1,1,4096,384]{3,2,1,0:T(8,128)(2,1)}, bf16[1,1,4096,384]{3,2,1,0:T(8,128)(2,1)}, bf16[1,1,384,4096]{3,2,1,0:T(8,128)(2,1)}) custom-call(bf16[1,64,4096]{2,1,0:T(8,128)(2,1)S(1)} %get-tuple-element.10.refs_0_, bf16[1,64,4096]{2,1,0:T(8,128)(2,1)S(1)} %get-tuple-element.11.refs_1_, ...), custom_call_target="tpu_custom_call" | custom-call | tf_op jit(solution)/shard_map/place/pallas_call | solution.py:466

commit v4 on v3

--- a/solution.py
+++ b/solution.py
@@ -66,12 +66,25 @@
     return pl.ds(pl.multiple_of(n * size, size), size)
 
 
+def combine(table_of, got, grads, out, h):
+    def body(g, total):
+        wanted = jnp.where(iota((2 * TOK, ALL), 0) < TOK, 0, g).astype(F32)
+        table = jnp.where(table_of[...] == wanted, 1.0, 0.0).astype(BF16)
+        value = mm(table, got[:, sent_cols(h, g)])
+        out[:, cols(h, g)] = (grads[:, cols(h, g)].astype(F32) + value[:TOK]).astype(BF16)
+        return total + value[TOK:]
+
+    total = lax.fori_loop(0, FULL, body, jnp.zeros((TOK, GROUP), F32))
+    tail = cols(h, FULL)
+    out[:, tail] = (grads[:, tail].astype(F32) + total).astype(BF16)
+
+
 def kernel(
     x_ref, dy_ref, last_ref, ids_ref, comb_ref, wg_ref, wu_ref, wd_ref,
-    first_ref, second_ref, gg_ref, gu_ref, gd_ref,
-    wgu, wd, xs, ws, gs, hs, g_far, h_far, send, back, got, dy_next,
-    pre, hg, key, key_t, comb_t, h_t,
-    ssem, rsem, wsem, pair_send, pair_recv, y_send, y_recv,
+    first_ref, gg_ref, gu_ref, gd_ref, got, dy_next, key,
+    x_in, dy_in, last_in, wgu, wd, xs, ws, gs, hs, g_far, h_far, send, back,
+    pre, hg, key_t, comb_t, h_t,
+    ssem, rsem, isem, wsem, pair_send, pair_recv, y_send, y_recv,
 ):
     section = lax.axis_index("section")
     place = lax.axis_index("expert")
@@ -94,13 +107,19 @@
     pl.semaphore_signal(barrier, inc=1, device_id=partner, device_id_type=MESH)
     pl.semaphore_signal(barrier, inc=1, device_id=after, device_id_type=MESH)
 
+    load = [
+        pltpu.make_async_copy(x_ref.at[0, 0], x_in.at[0], isem.at[0]),
+        pltpu.make_async_copy(dy_ref.at[0], dy_in, isem.at[1]),
+        pltpu.make_async_copy(x_ref.at[0, 1], x_in.at[1], isem.at[2]),
+        pltpu.make_async_copy(last_ref, last_in, isem.at[3]),
+    ]
+    load[0].start()
+
     own = [
         pltpu.make_async_copy(wg_ref.at[0, 0], gg_ref.at[0, 0], wsem.at[0]),
         pltpu.make_async_copy(wu_ref.at[0, 0], gu_ref.at[0, 0], wsem.at[1]),
         pltpu.make_async_copy(wd_ref.at[0, 0], gd_ref.at[0, 0], wsem.at[2]),
     ]
-    for copy in own:
-        copy.start()
 
     def tables(m):
         shape = (ALL, 2 * TOK)
@@ -128,7 +147,7 @@
         key[m] = value.T
         comb_t[m] = combined
 
-    def payload(m, source, scaled, buf, rows_ref, base, halves=BOTH):
+    def payload(m, source, scaled, buf, rows_ref, base, halves=BOTH, lo=0, count=ALL):
         def body(g, carry):
             data = jnp.concatenate(
                 [
@@ -137,14 +156,16 @@
                 ],
                 axis=0,
             )
-            lane = iota((ALL, 2 * TOK), 1)
+            lane = iota((count, 2 * TOK), 1)
+            rows = pl.ds(lo, count)
             wanted = jnp.where(lane < TOK, 0, g).astype(F32)
-            table = jnp.where(key_t[m] == wanted, comb_t[m] if scaled else 1.0, 0.0)
+            table = jnp.where(key_t[m, rows, :] == wanted, comb_t[m, rows, :] if scaled else 1.0, 0.0)
             value = mm(table.astype(BF16), data).astype(BF16)
             for n, h in enumerate(halves):
                 piece = value[:, n * GROUP : (n + 1) * GROUP]
-                send[buf, :, sent_cols(h, g)] = piece
-                rows_ref[pl.ds(base, ROWS), cols(h, g)] = piece[:ROWS]
+                send[buf, rows, sent_cols(h, g)] = piece
+                if lo == 0:
+                    rows_ref[pl.ds(base, ROWS), cols(h, g)] = piece[:ROWS]
             return carry
 
         lax.fori_loop(0, FULL, body, 0)
@@ -236,7 +257,7 @@
                 g_far[m, part, FF:] = up_rows
                 h_far[m, part, :] = hidden
 
-    def partials(m, lo, count, h):
+    def partials(m, lo, count, h, phase):
         def pair_of(n):
             part = cols(h, 2 * n, 2)
             own_part = jnp.concatenate([gg_ref[0, 0, part, :], gu_ref[0, 0, part, :]], axis=1)
@@ -253,52 +274,51 @@
         folded = last[:, GROUP:].astype(BF16)
         keep(6, last[:, :GROUP])
 
-        def body(n, carry):
+        def both(n):
             value = pair_of(n)
             keep(2 * n, value[:, :GROUP])
             keep(2 * n + 1, value[:, GROUP:])
-            return carry
-
-        lax.fori_loop(0, 3, body, 0)
-
-    def give_back(phase, slots, h):
-        for slot in slots:
+
+        both(2)
+        give_back(phase, h, 4, 3)
+        both(1)
+        both(0)
+        give_back(phase, h, 0, 4)
+
+    def give_back(phase, h, group, count):
+        for slot in OTHERS:
             pltpu.make_async_remote_copy(
-                src_ref=back.at[pl.ds(slot * ROWS, ROWS), sent_cols(h, 0, FULL)],
-                dst_ref=got.at[pl.ds(slot * ROWS, ROWS), sent_cols(h, 0, FULL)],
+                src_ref=back.at[pl.ds(slot * ROWS, ROWS), sent_cols(h, group, count)],
+                dst_ref=got.at[pl.ds(slot * ROWS, ROWS), sent_cols(h, group, count)],
                 send_sem=ssem.at[phase],
                 recv_sem=rsem.at[phase],
                 device_id=chip(slot, -1),
                 device_id_type=MESH,
             ).start()
 
-    def combine(m, grads, out, h):
-        def body(g, total):
-            wanted = jnp.where(iota((2 * TOK, ALL), 0) < TOK, 0, g).astype(F32)
-            table = jnp.where(key[m] == wanted, 1.0, 0.0).astype(BF16)
-            value = mm(table, got[:, sent_cols(h, g)])
-            out[0, :, cols(h, g)] = (grads[:, cols(h, g)].astype(F32) + value[:TOK]).astype(BF16)
-            return total + value[TOK:]
-
-        total = lax.fori_loop(0, FULL, body, jnp.zeros((TOK, GROUP), F32))
-        tail = cols(h, FULL)
-        out[0, :, tail] = (grads[:, tail].astype(F32) + total).astype(BF16)
-
     tables(0)
-    payload(0, x_ref.at[0, 0], False, 0, xs, 0)
+    load[0].wait()
+    for copy in load[1:] + own:
+        copy.start()
+    payload(0, x_in.at[0], False, 0, xs, 0, BOTH, 0, HALF)
     pl.semaphore_wait(barrier, PEERS + 1)
-    dispatch(0, 0, xs, 0, OTHERS)
+    dispatch(0, 0, xs, 0, EARLY)
+    payload(0, x_in.at[0], False, 0, xs, 0, BOTH, HALF, HALF)
+    dispatch(0, 0, xs, 0, LATE)
     far = [
         to_partner(0, wg_ref.at[0, 0], wgu.at[:, pl.ds(0, FF)]),
         to_partner(1, wu_ref.at[0, 0], wgu.at[:, pl.ds(FF, FF)]),
         to_partner(2, wd_ref.at[0, 0], wd),
     ]
+    load[1].wait()
+    payload(0, dy_in, True, 1, ws, 0)
+    dispatch(1, 1, ws, 0, OTHERS)
     for copy in far:
         copy.start()
-    payload(0, dy_ref.at[0], True, 1, ws, 0)
-    dispatch(1, 1, ws, 0, OTHERS)
     tables(1)
-    payload(1, x_ref.at[0, 1], False, 2, xs, 2 * ALL)
+    load[2].wait()
+    load[3].wait()
+    payload(1, x_in.at[1], False, 2, xs, 2 * ALL)
 
     for copy in own:
         copy.wait()
@@ -318,8 +338,7 @@
         hidden_part(0, 0, ALL, h)
     row_terms(0, 0, ALL)
     for h in BOTH:
-        partials(0, 0, ALL, h)
-        give_back(2 + h, OTHERS, h)
+        partials(0, 0, ALL, h, 2 + h)
     pair.append(to_partner(5, g_far.at[0], gs.at[rows_of(1), :]))
     pair[-1].start()
     pair.append(to_partner(6, h_far.at[0], hs.at[rows_of(1), :]))
@@ -339,32 +358,32 @@
 
         @pl.when(section == RING - 1)
         def _():
-            dy_next[:, cols(h, 0, 8)] = last_ref[:, cols(h, 0, 8)]
+            dy_next[:, cols(h, 0, 8)] = last_in[:, cols(h, 0, 8)]
 
         payload(1, dy_next, True, 0, ws, 2 * ALL, (h,))
 
+    dispatch(4, 2, xs, 2 * ALL, LATE)
     arrived(2, OTHERS, (0,))
-    combine(0, dy_ref.at[0], first_ref, 0)
+    combine(key.at[0], got, dy_in, first_ref.at[0], 0)
     relays[0].start()
     take(0)
     dispatch(5, 0, ws, 2 * ALL, OTHERS, (0,))
     arrived(3, OTHERS, (1,))
-    combine(0, dy_ref.at[0], first_ref, 1)
+    combine(key.at[0], got, dy_in, first_ref.at[0], 1)
     relays[1].start()
-    dispatch(4, 2, xs, 2 * ALL, LATE)
     take(1)
     dispatch(6, 0, ws, 2 * ALL, OTHERS, (1,))
 
     sent(2, OTHERS, (0,))
     sent(3, OTHERS, (1,))
+    arrived(5, OTHERS, (0,))
+    unfold(ws, 2 * ALL, ALL, (0,))
+    hidden_part(1, 0, ALL, 0)
     arrived(4)
     unfold(xs, 2 * ALL, ALL)
     pair.append(to_partner(7, xs.at[rows_of(2), :], xs.at[rows_of(3), :]))
     pair[-1].start()
     forward(1)
-    arrived(5, OTHERS, (0,))
-    unfold(ws, 2 * ALL, ALL, (0,))
-    hidden_part(1, 0, ALL, 0)
     arrived(6, OTHERS, (1,))
     unfold(ws, 2 * ALL, ALL, (1,))
     pair.append(to_partner(8, ws.at[rows_of(2), :], ws.at[rows_of(3), :]))
@@ -376,8 +395,7 @@
     pair.append(to_partner(10, h_far.at[1], hs.at[rows_of(3), :]))
     pair[-1].start()
     for h in BOTH:
-        partials(1, 0, ALL, h)
-        give_back(7 + h, OTHERS, h)
+        partials(1, 0, ALL, h, 8 + h)
 
     for copy in pair:
         copy.wait()
@@ -394,27 +412,33 @@
     lax.fori_loop(0, D // 512, weight_body, 0)
 
     for h in BOTH:
-        arrived(7 + h, OTHERS, (h,))
-        combine(1, dy_next, second_ref, h)
+        arrived(8 + h, OTHERS, (h,))
     sent(1)
     sent(4)
     sent(5, OTHERS, (0,))
     sent(6, OTHERS, (1,))
     for h in BOTH:
-        sent(7 + h, OTHERS, (h,))
-
-
-def place(*refs):
-    count = (len(refs) - 1) // 2
+        sent(8 + h, OTHERS, (h,))
+
+
+def finish(
+    first_ref, gg_ref, gu_ref, gd_ref, got, dy_next, key,
+    first_out, second_out, gg_out, gu_out, gd_out, second, sem,
+):
     copies = []
-    for source, result in zip(refs[:count], refs[count:-1]):
-        parts = 4 if source.size > 1 << 20 else 1
-        for p in range(parts):
-            size = source.shape[-2] // parts
-            rows = (0,) * (len(source.shape) - 2) + (pl.ds(p * size, size),)
-            copies.append(pltpu.make_async_copy(source.at[rows], result.at[rows], refs[-1].at[len(copies)]))
-    for copy in copies:
-        copy.start()
+
+    def write(source, result):
+        copies.append(pltpu.make_async_copy(source, result, sem.at[len(copies)]))
+        copies[-1].start()
+
+    for source, result in ((gg_ref, gg_out), (gu_ref, gu_out), (gd_ref, gd_out)):
+        for p in range(4):
+            rows = tile(p, source.shape[2] // 4)
+            write(source.at[0, 0, rows, :], result.at[0, 0, rows, :])
+    write(first_ref, first_out)
+    for h in BOTH:
+        combine(key.at[1], got, dy_next, second, h)
+        write(second.at[:, cols(h, 0, 8)], second_out.at[0, :, cols(h, 0, 8)])
     for copy in copies:
         copy.wait()
 
@@ -423,12 +447,17 @@
     vmem = pl.BlockSpec(memory_space=pltpu.VMEM)
     hbm = pl.BlockSpec(memory_space=pl.ANY)
     dma = pltpu.SemaphoreType.DMA
+    kept = [(a.shape, BF16) for a in (arriving, w_gate, w_up, w_down)]
+    kept += [((ALL, 2 * WIDE), BF16), ((TOK, D), BF16), ((2, 2 * TOK, ALL), F32)]
     results = pl.pallas_call(
         kernel,
-        out_shape=tuple(pltpu.VMEM(a.shape, BF16) for a in (arriving, arriving, w_gate, w_up, w_down)),
-        in_specs=[vmem] * 5 + [hbm] * 3,
-        out_specs=(vmem,) * 5,
+        out_shape=tuple(pltpu.VMEM(*k) for k in kept),
+        in_specs=[hbm] * 3 + [vmem] * 2 + [hbm] * 3,
+        out_specs=(vmem,) * 7,
         scratch_shapes=[
+            pltpu.VMEM((2, TOK, D), BF16),
+            pltpu.VMEM((TOK, D), BF16),
+            pltpu.VMEM((TOK, D), BF16),
             pltpu.VMEM((D, 2 * FF), BF16),
             pltpu.VMEM((FF, D), BF16),
             pltpu.VMEM((4 * ALL, D), BF16),
@@ -439,16 +468,14 @@
             pltpu.VMEM((2, ALL, FF), BF16),
             pltpu.VMEM((3, ALL, 2 * WIDE), BF16),
             pltpu.VMEM((ALL, 2 * WIDE), BF16),
-            pltpu.VMEM((ALL, 2 * WIDE), BF16),
-            pltpu.VMEM((TOK, D), BF16),
             pltpu.VMEM((2, ALL, 2 * FF), F32),
             pltpu.VMEM((ALL, 2 * FF), F32),
-            pltpu.VMEM((2, 2 * TOK, ALL), F32),
             pltpu.VMEM((2, ALL, 2 * TOK), F32),
             pltpu.VMEM((2, ALL, 2 * TOK), F32),
             pltpu.VMEM((FF, 4 * ALL), BF16),
-            dma((9,)),
-            dma((9,)),
+            dma((10,)),
+            dma((10,)),
+            dma((4,)),
             dma((3,)),
             dma((11,)),
             dma((11,)),
@@ -464,13 +491,15 @@
         combine.transpose(0, 3, 1, 2), w_gate, w_up, w_down,
     )
     return pl.pallas_call(
-        place,
-        out_shape=tuple(jax.ShapeDtypeStruct(r.shape, r.dtype) for r in results),
-        in_specs=[vmem] * 5,
+        finish,
+        out_shape=tuple(
+            jax.ShapeDtypeStruct(a.shape, BF16) for a in (arriving, arriving, w_gate, w_up, w_down)
+        ),
+        in_specs=[vmem] * 7,
         out_specs=(hbm,) * 5,
-        scratch_shapes=[dma((14,))],
-        compiler_params=pltpu.CompilerParams(vmem_limit_bytes=1 << 20),
-        name="place",
+        scratch_shapes=[pltpu.VMEM((TOK, D), BF16), dma((15,))],
+        compiler_params=pltpu.CompilerParams(vmem_limit_bytes=4 << 20),
+        name="write_results",
     )(*[pltpu.with_memory_space_constraint(r, pltpu.VMEM) for r in results])
 
 

time: 148 us -> 143 us (0.966)
  Pallas kernels: 147 us -> 142 us
    pallas_call x2, Pallas kernels: 147 us -> 142 us  [the longest x1 138 us: local(): pl.pallas_call(kernel, out_shape=tuple((pltpu.VMEM(*k) for k in kept)), i...]
where the time goes in v4:
time: 143 us; the launch traced here: 142 us
  Pallas kernels  142 us (99%)
    pallas_call x1, Pallas kernels, local(): pl.pallas_call(kernel, out_shape=tuple((pltpu.VMEM(*k) for k in kept)), i...  138 us
    pallas_call x1, Pallas kernels, local(): pl.pallas_call(finish, out_shape=tuple((jax.ShapeDtypeStruct(a.shape, BF1...  4.05 us

profile of v4, /device:TPU:16, one launch (start us, length us, event | category | flops | bytes accessed | tf_op | source)
XLA Modules:
  0.0 142.5 jit_solution(17359007234106819415)
XLA Ops:
  0.6 137.6 %relay_backward.1 = (bf16[1,64,4096]{2,1,0:T(8,128)(2,1)S(1)}, bf16[1,1,4096,384]{3,2,1,0:T(8,128)(2,1)S(1)}, bf16[1,1,4096,384]{3,2,1,0:T(8,128)(2,1)S(1)}, bf1...) custom-call(bf16[1,2,64,4096]{3,2,1,0:T(8,128)(2,1)} %x_ref.1, ...), custom_call_target="tpu_custom_call" | custom-call | tf_op jit(solution)/shard_map/relay_backward/pallas_call | solution.py:452
  138.3 4.0 %write_results.1 = (bf16[1,64,4096]{2,1,0:T(8,128)(2,1)}, bf16[1,64,4096]{2,1,0:T(8,128)(2,1)}, bf16[1,1,4096,384]{3,2,1,0:T(8,128)(2,1)}, bf16[1,1,4096,384]{3,2,1,0:T(8,128)(2,1)}, bf16[1,1,384,4096]{3,2,1,0:T(8,128)(2,1)}) custom-call(bf16[1,64,4096]{2,1,0:T(8,128)(2,1)S(1)} %get-tuple-element.12.first_ref, ...), custom_call_target="tpu_custom_call" | custom-call | tf_op jit(solution)/shard_map/write_results/pallas_call | solution.py:493

commit v5 on v4

--- a/solution.py
+++ b/solution.py
@@ -74,7 +74,7 @@
         out[:, cols(h, g)] = (grads[:, cols(h, g)].astype(F32) + value[:TOK]).astype(BF16)
         return total + value[TOK:]
 
-    total = lax.fori_loop(0, FULL, body, jnp.zeros((TOK, GROUP), F32))
+    total = lax.fori_loop(0, FULL, body, jnp.zeros((TOK, GROUP), F32), unroll=True)
     tail = cols(h, FULL)
     out[:, tail] = (grads[:, tail].astype(F32) + total).astype(BF16)
 
@@ -168,7 +168,7 @@
                     rows_ref[pl.ds(base, ROWS), cols(h, g)] = piece[:ROWS]
             return carry
 
-        lax.fori_loop(0, FULL, body, 0)
+        lax.fori_loop(0, FULL, body, 0, unroll=True)
 
     def dispatch(phase, buf, rows_ref, base, slots, halves=BOTH):
         for slot in slots:
@@ -320,6 +320,8 @@
     load[3].wait()
     payload(1, x_in.at[1], False, 2, xs, 2 * ALL)
 
+    dispatch(4, 2, xs, 2 * ALL, EARLY)
+
     for copy in own:
         copy.wait()
     for copy in far:
@@ -330,7 +332,7 @@
     pair[-1].start()
     forward(0)
     arrived(1)
-    dispatch(4, 2, xs, 2 * ALL, EARLY)
+    dispatch(4, 2, xs, 2 * ALL, LATE)
     unfold(ws, 0, ALL)
     pair.append(to_partner(4, ws.at[rows_of(0), :], ws.at[rows_of(1), :]))
     pair[-1].start()
@@ -362,7 +364,6 @@
 
         payload(1, dy_next, True, 0, ws, 2 * ALL, (h,))
 
-    dispatch(4, 2, xs, 2 * ALL, LATE)
     arrived(2, OTHERS, (0,))
     combine(key.at[0], got, dy_in, first_ref.at[0], 0)
     relays[0].start()

time: 143 us -> 141 us (0.986)
  Pallas kernels: 142 us -> 140 us
    pallas_call x1, Pallas kernels: 138 us -> 136 us  [local(): pl.pallas_call(kernel, out_shape=tuple((pltpu.VMEM(*k) for k in kept)), i...]
where the time goes in v5:
time: 141 us
  Pallas kernels  140 us (99%)
    pallas_call x1, Pallas kernels, local(): pl.pallas_call(kernel, out_shape=tuple((pltpu.VMEM(*k) for k in kept)), i...  136 us
    pallas_call x1, Pallas kernels, local(): pl.pallas_call(finish, out_shape=tuple((jax.ShapeDtypeStruct(a.shape, BF1...  4.05 us

profile of v5, /device:TPU:16, one launch (start us, length us, event | category | flops | bytes accessed | tf_op | source)
XLA Modules:
  0.0 140.5 jit_solution(3304974714798893977)
XLA Ops:
  0.6 135.6 %relay_backward.1 = (bf16[1,64,4096]{2,1,0:T(8,128)(2,1)S(1)}, bf16[1,1,4096,384]{3,2,1,0:T(8,128)(2,1)S(1)}, bf16[1,1,4096,384]{3,2,1,0:T(8,128)(2,1)S(1)}, bf1...) custom-call(bf16[1,2,64,4096]{3,2,1,0:T(8,128)(2,1)} %x_ref.1, ...), custom_call_target="tpu_custom_call" | custom-call | tf_op jit(solution)/shard_map/relay_backward/pallas_call | solution.py:453
  136.3 4.1 %write_results.1 = (bf16[1,64,4096]{2,1,0:T(8,128)(2,1)}, bf16[1,64,4096]{2,1,0:T(8,128)(2,1)}, bf16[1,1,4096,384]{3,2,1,0:T(8,128)(2,1)}, bf16[1,1,4096,384]{3,2,1,0:T(8,128)(2,1)}, bf16[1,1,384,4096]{3,2,1,0:T(8,128)(2,1)}) custom-call(bf16[1,64,4096]{2,1,0:T(8,128)(2,1)S(1)} %get-tuple-element.12.first_ref, ...), custom_call_target="tpu_custom_call" | custom-call | tf_op jit(solution)/shard_map/write_results/pallas_call | solution.py:494

commit v6 on v5

--- a/solution.py
+++ b/solution.py
@@ -66,15 +66,16 @@
     return pl.ds(pl.multiple_of(n * size, size), size)
 
 
-def combine(table_of, got, grads, out, h):
-    def body(g, total):
+def combine(table_of, got, grads, out, h, midway=None):
+    total = jnp.zeros((TOK, GROUP), F32)
+    for g in range(FULL):
         wanted = jnp.where(iota((2 * TOK, ALL), 0) < TOK, 0, g).astype(F32)
         table = jnp.where(table_of[...] == wanted, 1.0, 0.0).astype(BF16)
         value = mm(table, got[:, sent_cols(h, g)])
         out[:, cols(h, g)] = (grads[:, cols(h, g)].astype(F32) + value[:TOK]).astype(BF16)
-        return total + value[TOK:]
-
-    total = lax.fori_loop(0, FULL, body, jnp.zeros((TOK, GROUP), F32), unroll=True)
+        total = total + value[TOK:]
+        if g == 3 and midway is not None:
+            midway()
     tail = cols(h, FULL)
     out[:, tail] = (grads[:, tail].astype(F32) + total).astype(BF16)
 
@@ -349,14 +350,16 @@
 
     relays = [
         pltpu.make_async_remote_copy(
-            src_ref=first_ref.at[0, :, cols(h, 0, 8)], dst_ref=dy_next.at[:, cols(h, 0, 8)],
-            send_sem=y_send.at[h], recv_sem=y_recv.at[h], device_id=before, device_id_type=MESH,
+            src_ref=first_ref.at[0, :, cols(q // 2, q % 2 * 4, 4)],
+            dst_ref=dy_next.at[:, cols(q // 2, q % 2 * 4, 4)],
+            send_sem=y_send.at[q], recv_sem=y_recv.at[q], device_id=before, device_id_type=MESH,
         )
-        for h in BOTH
+        for q in range(4)
     ]
 
     def take(h):
-        relays[h].wait()
+        relays[2 * h].wait()
+        relays[2 * h + 1].wait()
 
         @pl.when(section == RING - 1)
         def _():
@@ -365,13 +368,13 @@
         payload(1, dy_next, True, 0, ws, 2 * ALL, (h,))
 
     arrived(2, OTHERS, (0,))
-    combine(key.at[0], got, dy_in, first_ref.at[0], 0)
-    relays[0].start()
+    combine(key.at[0], got, dy_in, first_ref.at[0], 0, relays[0].start)
+    relays[1].start()
     take(0)
     dispatch(5, 0, ws, 2 * ALL, OTHERS, (0,))
     arrived(3, OTHERS, (1,))
-    combine(key.at[0], got, dy_in, first_ref.at[0], 1)
-    relays[1].start()
+    combine(key.at[0], got, dy_in, first_ref.at[0], 1, relays[2].start)
+    relays[3].start()
     take(1)
     dispatch(6, 0, ws, 2 * ALL, OTHERS, (1,))
 
@@ -480,8 +483,8 @@
             dma((3,)),
             dma((11,)),
             dma((11,)),
-            dma((2,)),
-            dma((2,)),
+            dma((4,)),
+            dma((4,)),
         ],
         compiler_params=pltpu.CompilerParams(
             collective_id=0, has_side_effects=True, vmem_limit_bytes=50 << 20

time: 141 us -> 141 us (level)
  no operation moved by 1% of the time
where the time goes in v6:
time: 141 us
  Pallas kernels  140 us (99%)
    pallas_call x1, Pallas kernels, local(): pl.pallas_call(kernel, out_shape=tuple((pltpu.VMEM(*k) for k in kept)), i...  136 us
    pallas_call x1, Pallas kernels, local(): pl.pallas_call(finish, out_shape=tuple((jax.ShapeDtypeStruct(a.shape, BF1...  4.05 us

profile of v6, /device:TPU:16, one launch (start us, length us, event | category | flops | bytes accessed | tf_op | source)
XLA Modules:
  0.0 140.5 jit_solution(14270855070164400342)
XLA Ops:
  0.6 135.7 %relay_backward.1 = (bf16[1,64,4096]{2,1,0:T(8,128)(2,1)S(1)}, bf16[1,1,4096,384]{3,2,1,0:T(8,128)(2,1)S(1)}, bf16[1,1,4096,384]{3,2,1,0:T(8,128)(2,1)S(1)}, bf1...) custom-call(bf16[1,2,64,4096]{3,2,1,0:T(8,128)(2,1)} %x_ref.1, ...), custom_call_target="tpu_custom_call" | custom-call | tf_op jit(solution)/shard_map/relay_backward/pallas_call | solution.py:456
  136.3 4.1 %write_results.1 = (bf16[1,64,4096]{2,1,0:T(8,128)(2,1)}, bf16[1,64,4096]{2,1,0:T(8,128)(2,1)}, bf16[1,1,4096,384]{3,2,1,0:T(8,128)(2,1)}, bf16[1,1,4096,384]{3,2,1,0:T(8,128)(2,1)}, bf16[1,1,384,4096]{3,2,1,0:T(8,128)(2,1)}) custom-call(bf16[1,64,4096]{2,1,0:T(8,128)(2,1)S(1)} %get-tuple-element.12.first_ref, ...), custom_call_target="tpu_custom_call" | custom-call | tf_op jit(solution)/shard_map/write_results/pallas_call | solution.py:497
